TPU v7x, 32 devices: a whole 2x2x4 slice. The times are simulated.
32 devices in a mesh: section: 4 (over x, core), dp: 8 (over z, y).
Axes of the slice: x: 2, y: 2, z: 4, core: 2. Of those that a mesh axis runs over, the one named last changes fastest.
Arguments:
- layer_input: bfloat16 [4, 2, 2048, 4096], P('section', None, 'dp'), may hold values from -6 to 6
- queries: bfloat16 [4, 2, 2048, 4096], P('section', None, 'dp'), may hold values from -85 to 85
- attn_grad: bfloat16 [4, 2, 2048, 4096], P('section', None, 'dp'), may hold values from -6 to 6
- top_grad: bfloat16 [2, 2048, 4096], P(None, 'dp', 'section'), may hold values from -6 to 6
- positions: int32 [2, 2048], P(None, 'dp'), may hold values from 0 to 255, as said below
- norm_gain: float32 [4, 4096], P('section'), may hold values from 0.1 to 1.9
- key_weight: bfloat16 [4, 4096, 512], P('section'), may hold values from -0.09375 to 0.09375
- value_weight: bfloat16 [4, 4096, 512], P('section'), may hold values from -0.09375 to 0.09375
Outputs:
- passed_grad: bfloat16 [4, 2, 2048, 4096], P('section', None, 'dp')
- key_grad: float32 [4, 4096, 512], P('section', 'dp')
- value_grad: float32 [4, 4096, 512], P('section', 'dp')
- gain_grad: float32 [4, 4096], P('section', 'dp')
Inputs may be any that keep to these rules, and one draw needn't show every extreme that they name: `positions`: within each block of 256 tokens the first position is 0; each later position is 0 (a new document) or one more than the previous one. In each micro-batch the first block of 256 tokens is a single document.
All inputs are finite; a program needn't handle non-finite values.
Results may differ from a plain program's by a relative error of at most 0.0095.
The roundings to bfloat16 on the way count: a program that leaves them out, or rounds other values in their place, can miss the bound.
Values may be sent and summed in bfloat16 or wider, within the bound.
A program may use at most 192 MiB of HBM per device.

v0:
```python
import jax
import jax.numpy as jnp
from jax import lax
from jax.sharding import PartitionSpec as P

HD = 128
KV = 4
GRP = 8


EPS = 1e-05


def passed_along(value, axis, steps):
    count = lax.axis_size(axis)
    first, last = (max(0, -steps), min(count, count - steps))
    return lax.ppermute(value, axis, [(source, source + steps) for source in range(first, last)])


def add_triple(former, latter):
    return tuple((first_item + second_item for first_item, second_item in zip(former, latter)))


def section_terms(hidden_rows, query_rows, grad_rows, places, gain_row, w_key, w_value):
    length, width = hidden_rows.shape
    values_f = hidden_rows.astype(jnp.float32)
    inverse = lax.rsqrt(jnp.mean(values_f * values_f, axis=-1, keepdims=True) + EPS)
    unit_rows = values_f * inverse
    normed = (unit_rows * gain_row).astype(jnp.bfloat16)
    key_flat = jnp.dot(normed, w_key, preferred_element_type=jnp.float32).astype(jnp.bfloat16)
    value_flat = jnp.dot(normed, w_value, preferred_element_type=jnp.float32).astype(jnp.bfloat16)
    key_heads = key_flat.reshape(length, KV, HD)
    value_heads = value_flat.reshape(length, KV, HD)
    query_heads = query_rows.reshape(length, KV, GRP, HD)
    grad_heads = grad_rows.reshape(length, KV, GRP, HD)
    score_scale = HD ** (-0.5)
    scores = (
        jnp.einsum("qgjd,kgd->gjqk", query_heads, key_heads, preferred_element_type=jnp.float32)
        * score_scale
    )
    position = jnp.arange(length, dtype=jnp.int32)
    distance = position[:, None] - position[None, :]
    allowed = (distance >= 0) & (distance <= places[:, None])
    scores = jnp.where(allowed[None, None], scores, jnp.float32(-1e30))
    probs = jax.nn.softmax(scores, axis=-1)
    probs_b = probs.astype(jnp.bfloat16)
    dprobs = jnp.einsum(
        "qgjd,kgd->gjqk", grad_heads, value_heads, preferred_element_type=jnp.float32
    )
    row_total = jnp.sum(probs * dprobs, axis=-1, keepdims=True)
    dscores = (probs * (dprobs - row_total)).astype(jnp.bfloat16)
    dkeys = (
        jnp.einsum("gjqk,qgjd->kgd", dscores, query_heads, preferred_element_type=jnp.float32)
        * score_scale
    ).astype(jnp.bfloat16)
    dvalues = jnp.einsum(
        "gjqk,qgjd->kgd", probs_b, grad_heads, preferred_element_type=jnp.float32
    ).astype(jnp.bfloat16)
    dkeys = dkeys.reshape(length, KV * HD)
    dvalues = dvalues.reshape(length, KV * HD)
    back_dims = (((1,), (1,)), ((), ()))
    dnormed = lax.dot_general(dkeys, w_key, back_dims, preferred_element_type=jnp.float32)
    dnormed = dnormed + lax.dot_general(
        dvalues, w_value, back_dims, preferred_element_type=jnp.float32
    )
    gain_term = jnp.sum(dnormed * unit_rows, axis=0)
    dunit = dnormed * gain_row
    branch = inverse * (dunit - unit_rows * jnp.mean(dunit * unit_rows, axis=-1, keepdims=True))
    row_dims = (((0,), (0,)), ((), ()))
    key_term = lax.dot_general(normed, dkeys, row_dims, preferred_element_type=jnp.float32)
    value_term = lax.dot_general(normed, dvalues, row_dims, preferred_element_type=jnp.float32)
    return (branch, key_term, value_term, gain_term)


def relay_step(incoming, branch, top_part, is_last):
    base = jnp.where(is_last, top_part, incoming.astype(jnp.float32))
    return (base + branch).astype(jnp.bfloat16)


def shards(
    layer_input, queries, attn_grad, top_grad, positions, norm_gain, key_weight, value_weight
):
    micro_count = layer_input.shape[1]
    seq_total = micro_count * lax.axis_size("dp")
    gain_row = norm_gain[0]
    branch_list = []
    shares = None
    summed = None
    for micro_index in range(micro_count):
        branch, key_term, value_term, gain_term = section_terms(
            layer_input[0, micro_index],
            queries[0, micro_index],
            attn_grad[0, micro_index],
            positions[micro_index],
            gain_row,
            key_weight[0],
            value_weight[0],
        )
        branch_list.append(branch)
        micro_terms = (key_term, value_term, gain_term)
        summed = micro_terms if summed is None else add_triple(summed, micro_terms)
    shares = lax.psum_scatter(summed, "dp", scatter_dimension=0, tiled=True)
    stacked = jnp.stack(branch_list)
    top_full = lax.all_gather(top_grad, "section", axis=2, tiled=True).astype(jnp.float32)
    is_last = lax.axis_index("section") == lax.axis_size("section") - 1
    hop_count = lax.axis_size("section") - 1
    passed = relay_step(jnp.zeros(stacked.shape, jnp.bfloat16), stacked, top_full, is_last)
    for hop_index in range(hop_count):
        passed = relay_step(passed_along(passed, "section", -1), stacked, top_full, is_last)
    key_share = shares[0] / seq_total
    value_share = shares[1] / seq_total
    gain_share = shares[2] / seq_total
    return (passed[None], key_share[None], value_share[None], gain_share[None])


def solution(mesh):
    return jax.shard_map(
        shards,
        mesh=mesh,
        in_specs=(
            P("section", None, "dp", None),
            P("section", None, "dp", None),
            P("section", None, "dp", None),
            P(None, "dp", "section"),
            P(None, "dp"),
            P("section", None),
            P("section", None, None),
            P("section", None, None),
        ),
        out_specs=(
            P("section", None, "dp", None),
            P("section", "dp", None),
            P("section", "dp", None),
            P("section", "dp"),
        ),
        check_vma=False,
    )
```

profile of v0, /device:TPU:1, one launch (start us, length us, event | category | flops | bytes accessed | tf_op | source)
XLA Modules:
  0.0 421.9 jit_solution(18313226744337225412)
XLA Ops:
  8.8 3.3 fusion.33
  12.2 3.7 fusion.104
  15.9 1.3 fusion.110
  18.1 1.3 fusion.101
  19.4 1.3 fusion.107
  20.7 1.3 copy-done.13
  22.0 2.3 fusion.147
  24.3 3.8 copy.82
  28.2 4.8 %fusion.146 = (bf16[1,1,256,4096]{3,2,1,0:T(8,128)(2,1)}, bf16[1,1,256,4096]{3,2,1,0:T(8,128)(2,1)}) fusion(bf16[1,2,256,4096]{3,2,1,0:T(8,128)(2,1)} %param.10), kind=kLoop, calls=%fused_computation.139 | loop fusion | bytes 8388608 | tf_op jit(solution)/shard_map/slice | solution.py:93
  33.0 4.1 copy.80
  37.2 4.1 copy.81
  41.4 4.5 %fusion.121 = f32[4,256,256,8]{2,1,3,0:T(8,128)} fusion(bf16[256,4,8,128]{0,3,2,1:T(8,128)(2,1)S(1)} %bitcast.217, bf16[256,4,128,1]{2,1,0,3:T(4,128)(2,1)S(1)} %bitcast.241), kind=kOutput, calls=%fused_computation.116 | convolution fusion | flops 536870912 | bytes 10747904 | tf_op jit(solution)/shard_map/qgjd,kgd->gjqk/dot_general | solution.py:38
  45.9 1.2 fusion.125
  47.1 2.4 fusion.149
  49.5 4.9 %fusion.13 = (f32[4,8,256]{2,1,0:T(8,128)S(1)}, f32[4,256,256,8]{2,1,3,0:T(8,128)}) fusion(f32[4,8,256,256]{2,3,1,0:T(8,128)S(1)} %get-tuple-element.21, f32[4,8,256]{2,1,0:T(8,128)S(1)} %get-tuple-element.20, bf16[256,4,8,128]{0,3,2,1:T(8,128)(2,1)S(1)} %bitcast.221, bf16[256,4,128,1]{2,1,0,3:T(4,128)(2,1)S(1)} %bitcast.246), kind=kOutput, calls=%fused_computation.23 | convolution fusion | flops 543154176 | bytes 19202048 | tf_op jit(solution)/shard_map/qgjd,kgd->gjqk/dot_general | solution.py:47
  54.4 0.9 copy-done.22
  55.4 4.2 %copy.83 = bf16[1,1,256,4096]{2,3,1,0:T(8,128)(2,1)} copy(bf16[1,1,256,4096]{3,2,1,0:T(8,128)(2,1)} %get-tuple-element.15) | data formatting | bytes 4194304
  59.7 8.1 %fusion.116 = bf16[4,256,128]{1,2,0:T(8,128)(2,1)S(1)} fusion(bf16[256,4,8,128]{0,3,2,1:T(8,128)(2,1)} %bitcast.219, f32[4,256,256,8]{2,1,3,0:T(8,128)} %get-tuple-element.23, f32[4,8,256]{2,1,0:T(8,128)S(1)} %get-tuple-element.22, f32[4,8,256,256]{2,3,1,0:T(8,128)} %copy-done.22, f32[4,8,256]{2,1,0:T(8,128)S(1)} %get-tuple-element.20), kind=kOutput, calls=%fused_computation.111 | convolution fusion | flops 545521664 | bytes 19202048 | tf_op jit(solution)/shard_map/gjqk,qgjd->kgd/dot_general | solution.py:53
  67.8 4.7 %fusion.138 = f32[4096,512]{1,0:T(8,128)} fusion(bf16[256,512]{0,1:T(8,128)(2,1)S(1)} %bitcast.235, f32[4096]{0:T(1024)S(1)} %bitcast.229, f32[256]{0:T(256)S(1)} %get-tuple-element.30, bf16[1,2,256,4096]{3,2,1,0:T(8,128)(2,1)S(1)} %copy-done.1), kind=kOutput, calls=%fused_computation.138 | convolution fusion | flops 1077936128 | bytes 10765312 | tf_op jit(solution)/shard_map/dot_general | solution.py:70
  72.4 9.1 %fusion.150 = (f32[4,8,256]{2,1,0:T(8,128)S(1)}, f32[4,8,256,256]{2,3,1,0:T(8,128)S(1)}) fusion(f32[4,256,256,8]{2,1,3,0:T(8,128)} %fusion.121, pred[256,256]{0,1:T(8,128)(4,1)S(1)} %fusion.130), kind=kOutput, calls=%fused_computation.143 | output fusion | flops 12583167 | bytes 16875520 | tf_op jit(solution)/shard_map/sub | solution.py:45
  81.6 4.9 %fusion.10 = (f32[4,8,256]{2,1,0:T(8,128)S(1)}, f32[4,256,256,8]{2,1,3,0:T(8,128)}) fusion(f32[4,8,256,256]{2,3,1,0:T(8,128)S(1)} %get-tuple-element.25, f32[4,8,256]{2,1,0:T(8,128)S(1)} %get-tuple-element.24, bf16[256,4,8,128]{0,3,2,1:T(8,128)(2,1)S(1)} %bitcast.223, bf16[256,4,128,1]{2,1,0,3:T(4,128)(2,1)S(1)} %bitcast.245), kind=kOutput, calls=%fused_computation.17 | convolution fusion | flops 543154176 | bytes 19202048 | tf_op jit(solution)/shard_map/qgjd,kgd->gjqk/dot_general | solution.py:47
  87.3 7.3 %fusion.113 = bf16[4,256,128]{1,2,0:T(8,128)(2,1)S(1)} fusion(bf16[256,4,8,128]{0,3,2,1:T(8,128)(2,1)S(1)} %bitcast.218, f32[4,256,256,8]{2,1,3,0:T(8,128)} %get-tuple-element.27, f32[4,8,256]{2,1,0:T(8,128)S(1)} %get-tuple-element.26, f32[4,8,256,256]{2,3,1,0:T(8,128)} %copy-done.23, f32[4,8,256]{2,1,0:T(8,128)S(1)} %get-tuple-element.24), kind=kOutput, calls=%fused_computation.110 | convolution fusion | flops 545521664 | bytes 19202048 | tf_op jit(solution)/shard_map/gjqk,qgjd->kgd/dot_general | solution.py:53
  94.7 8.1 %convolution_add_fusion.1 = f32[4096,512]{1,0:T(8,128)} fusion(f32[4096,512]{1,0:T(8,128)} %fusion.138, bf16[256,512]{0,1:T(8,128)(2,1)S(1)} %bitcast.237, f32[256]{0:T(256)S(1)} %get-tuple-element.29, f32[4096]{0:T(1024)S(1)} %bitcast.230, bf16[1,2,256,4096]{3,2,1,0:T(8,128)(2,1)S(1)} %copy-done.1), kind=kOutput, calls=%fused_computation.30 | convolution fusion | flops 1080033280 | bytes 19153920 | tf_op jit(solution)/shard_map/dot_general | solution.py:70
  103.1 1.3 copy-done.16
  104.4 5.0 %fusion.98 = bf16[4,256,128]{1,2,0:T(8,128)(2,1)S(1)} fusion(bf16[256,4,8,128]{0,3,2,1:T(8,128)(2,1)S(1)} %bitcast.222, f32[4,8,256,256]{2,3,1,0:T(8,128)} %copy-done.22, f32[4,8,256]{2,1,0:T(8,128)S(1)} %get-tuple-element.20), kind=kOutput, calls=%fused_computation.105 | convolution fusion | flops 541196288 | bytes 10780672 | tf_op jit(solution)/shard_map/gjqk,qgjd->kgd/dot_general | solution.py:56
  109.5 1.4 fusion.136
  111.1 5.6 %fusion.95 = bf16[4,256,128]{1,2,0:T(8,128)(2,1)S(1)} fusion(bf16[256,4,8,128]{0,3,2,1:T(8,128)(2,1)S(1)} %bitcast.224, f32[4,8,256,256]{2,3,1,0:T(8,128)} %copy-done.23, f32[4,8,256]{2,1,0:T(8,128)S(1)} %get-tuple-element.24), kind=kOutput, calls=%fused_computation.104 | convolution fusion | flops 541196288 | bytes 10780672 | tf_op jit(solution)/shard_map/gjqk,qgjd->kgd/dot_general | solution.py:56
  116.7 4.7 %convolution_add_fusion = f32[4096,512]{1,0:T(8,128)} fusion(f32[4096,512]{1,0:T(8,128)S(1)} %fusion.136, bf16[256,512]{0,1:T(8,128)(2,1)S(1)} %bitcast.239, f32[256]{0:T(256)S(1)} %get-tuple-element.29, f32[4096]{0:T(1024)S(1)} %bitcast.232, bf16[1,2,256,4096]{3,2,1,0:T(8,128)(2,1)S(1)} %copy-done.2), kind=kOutput, calls=%fused_computation.29 | convolution fusion | flops 1080033280 | bytes 19153920 | tf_op jit(solution)/shard_map/dot_general | solution.py:71
  121.4 5.7 %fusion.55 = f32[256,4096]{1,0:T(8,128)} fusion(bf16[256,512]{0,1:T(8,128)(2,1)S(1)} %bitcast.238, bf16[1,4096,512]{2,1,0:T(8,128)(2,1)} %param.14), kind=kOutput, calls=%fused_computation.74 | convolution fusion | flops 1073741824 | bytes 8650752 | tf_op jit(solution)/shard_map/dot_general | solution.py:62
  127.1 3.3 fusion.59
  130.4 5.0 %convolution_add_fusion.2 = f32[256,4096]{1,0:T(8,128)S(1)} fusion(f32[256,4096]{1,0:T(8,128)} %fusion.55, bf16[256,512]{0,1:T(8,128)(2,1)S(1)} %bitcast.240, bf16[1,4096,512]{2,1,0:T(8,128)(2,1)} %param.15), kind=kOutput, calls=%fused_computation.33 | convolution fusion | flops 1074790400 | bytes 12845056 | tf_op jit(solution)/shard_map/dot_general | solution.py:63
  135.4 1.0 copy-done.12
  136.4 1.3 copy-done.14
  137.7 5.9 %fusion.32 = (f32[4096]{0:T(1024)S(1)}, f32[256]{0:T(256)S(1)}, f32[256]{0:T(256)S(1)}, f32[4096]{0:T(1024)S(1)}, f32[256,4096]{1,0:T(8,128)}) fusion(f32[256]{0:T(256)S(1)} %get-tuple-element.30, bf16[1,2,256,4096]{3,2,1,0:T(8,128)(2,1)S(1)} %copy-done.3, f32[4096]{0:T(1024)S(1)} %bitcast.233, f32[256]{0:T(256)S(1)} %get-tuple-element.29, ...), kind=kOutput, calls=%fused_computation.53 | convolution fusion | flops 1089461760 | bytes 21286912 | tf_op jit(solution)/shard_map/dot_general | solution.py:63
  143.6 8.3 %fusion.31 = (f32[1,256,4096]{2,1,0:T(8,128)}, f32[1,256,4096]{2,1,0:T(8,128)}) fusion(f32[256,4096]{1,0:T(8,128)} %get-tuple-element.28, f32[256]{0:T(256)S(1)} %broadcast_multiply_fusion.1, f32[4096]{0:T(1024)S(1)} %bitcast.234, f32[256]{0:T(256)S(1)} %get-tuple-element.30, bf16[1,2,256,4096]{3,2,1,0:T(8,128)(2,1)} %param.8, ...), kind=kLoop, calls=%fused_computation.52 | loop fusion | flops 12582912 | bytes 20992000 | tf_op jit(solution)/shard_map/stack | solution.py:103
  151.9 5.5 %fusion.3 = bf16[2,256,4096]{2,1,0:T(8,128)(2,1)S(1)} fusion(bf16[2,256,4096]{2,1,0:T(8,128)(2,1)} %all-gather.2.cloned.1.call-done, pred[]{:T(512)S(6)} %eq.3, f32[1,256,4096]{2,1,0:T(8,128)} %get-tuple-element.13, f32[1,256,4096]{2,1,0:T(8,128)} %get-tuple-element.12), kind=kLoop, calls=%fused_computation.7 | loop fusion | flops 10485760 | bytes 16777216 | tf_op jit(solution)/shard_map/convert_element_type | solution.py:77
  157.4 2.3 collective-permute-start
  159.8 49.0 %collective-permute-done = bf16[2,256,4096]{2,1,0:T(8,128)(2,1)S(1)} collective-permute-done((bf16[2,256,4096]{2,1,0:T(8,128)(2,1)S(1)}, bf16[2,256,4096]{2,1,0:T(8,128)(2,1)S(1)}, u32[]{:S(2)}, u32[]{:S(2)}) %collective-permute-start) | collective-permute-done | bytes 4194336 | tf_op jit(solution)/shard_map/ppermute | solution.py:17
  208.7 2.1 fusion.5
  210.8 1.9 collective-permute-start.1
  212.8 47.9 %collective-permute-done.1 = bf16[2,256,4096]{2,1,0:T(8,128)(2,1)S(1)} collective-permute-done((bf16[2,256,4096]{2,1,0:T(8,128)(2,1)S(1)}, bf16[2,256,4096]{2,1,0:T(8,128)(2,1)S(1)}, u32[]{:S(2)}, u32[]{:S(2)}) %collective-permute-start.1) | collective-permute-done | bytes 4194336 | tf_op jit(solution)/shard_map/ppermute | solution.py:17
  260.7 3.2 fusion.7
  263.9 1.9 collective-permute-start.2
  267.1 32.4 %all-reduce = f32[4096]{0:T(1024)S(1)} all-reduce(f32[4096]{0:T(1024)S(1)} %add.59), channel_id=4, replica_groups=mesh['section'=4,'dp'=8] {'dp'}, use_global_device_ids=true, to_apply=%region_14.15.clone | all-reduce | flops 4096 | bytes 32768
  300.1 2.4 multiply_bitcast_fusion.1
  302.6 100.4 %reduce-scatter.5.cloned.1.call-done = f32[512,512]{1,0:T(8,128)} async-done(((f32[4096,512]{1,0:T(8,128)}), f32[512,512]{1,0:T(8,128)}) %reduce-scatter.5.cloned.1.call-update) | async-done | bytes 1048592 | tf_op jit(solution)/shard_map/reduce_scatter | solution.py:102
  403.0 2.3 multiply_bitcast_fusion
  405.3 8.9 %fusion.48 = bf16[1,2,256,4096]{3,2,1,0:T(8,128)(2,1)} fusion(bf16[2,256,4096]{2,1,0:T(8,128)(2,1)} %collective-permute-done.2, bf16[2,256,4096]{2,1,0:T(8,128)(2,1)} %all-gather.2.cloned.1.call-done, pred[]{:T(512)S(6)} %eq.3, f32[1,256,4096]{2,1,0:T(8,128)} %get-tuple-element.13, f32[1,256,4096]{2,1,0:T(8,128)} %get-tuple-element.12), kind=kLoop, calls=%fused_computation.67 | loop fusion | flops 12582912 | bytes 20971520 | tf_op jit(solution)/shard_map/broadcast_in_dim | solution.py:113
  (65 shorter events, 4.8 us)
Async XLA Ops:
  8.0 4.1 copy-start.19
  8.0 143.9 %all-gather.2.cloned.1.call-start = ((), (), s32[]{:S(2)}) async-start(), calls=%async_computation.2 | async-start | bytes 5242880 | tf_op jit(solution)/shard_map/all_gather | solution.py:104
  8.7 291.4 %reduce-scatter.3.cloned.1.call-start = ((), (), s32[]{:S(2)}) async-start(), calls=%async_computation.3 | async-start | bytes 9437184 | tf_op jit(solution)/shard_map/reduce_scatter | solution.py:102
  8.8 3.5 copy-start
  12.2 3.7 copy-start.11
  15.9 2.2 copy-start.8
  19.4 2.6 copy-start.13
  24.3 3.9 copy-start.20
  41.4 4.5 %copy-start.10 = (bf16[1,1,256,4096]{2,3,1,0:T(8,128)(2,1)S(1)}, bf16[1,1,256,4096]{2,3,1,0:T(8,128)(2,1)}, u32[]{:S(2)}) copy-start(bf16[1,1,256,4096]{2,3,1,0:T(8,128)(2,1)} %copy.80) | copy-start | bytes 6291460
  47.1 2.4 copy-start.15
  49.5 5.9 %copy-start.22 = (f32[4,8,256,256]{2,3,1,0:T(8,128)}, f32[4,8,256,256]{2,3,1,0:T(8,128)S(1)}, u32[]{:S(2)}) copy-start(f32[4,8,256,256]{2,3,1,0:T(8,128)S(1)} %get-tuple-element.21) | copy-start | bytes 25165828
  59.7 8.1 %copy-start.1 = (bf16[1,2,256,4096]{3,2,1,0:T(8,128)(2,1)S(1)}, bf16[1,2,256,4096]{3,2,1,0:T(8,128)(2,1)}, u32[]{:S(2)}) copy-start(bf16[1,2,256,4096]{3,2,1,0:T(8,128)(2,1)} %param.8) | copy-start | bytes 12582916
  72.4 9.1 %copy-start.17 = (bf16[1,1,256,4096]{2,3,1,0:T(8,128)(2,1)S(1)}, bf16[1,1,256,4096]{2,3,1,0:T(8,128)(2,1)}, u32[]{:S(2)}) copy-start(bf16[1,1,256,4096]{2,3,1,0:T(8,128)(2,1)} %copy.83) | copy-start | bytes 6291460
  81.6 5.8 %copy-start.23 = (f32[4,8,256,256]{2,3,1,0:T(8,128)}, f32[4,8,256,256]{2,3,1,0:T(8,128)S(1)}, u32[]{:S(2)}) copy-start(f32[4,8,256,256]{2,3,1,0:T(8,128)S(1)} %get-tuple-element.25) | copy-start | bytes 25165828
  102.8 1.6 copy-start.16
  102.8 300.2 %reduce-scatter.5.cloned.1.call-start = ((), (), s32[]{:S(2)}) async-start(), calls=%async_computation.4 | async-start | bytes 9437184 | tf_op jit(solution)/shard_map/reduce_scatter | solution.py:102
  104.4 5.1 %copy-start.2 = (bf16[1,2,256,4096]{3,2,1,0:T(8,128)(2,1)S(1)}, bf16[1,2,256,4096]{3,2,1,0:T(8,128)(2,1)}, u32[]{:S(2)}) copy-start(bf16[1,2,256,4096]{3,2,1,0:T(8,128)(2,1)} %param.8) | copy-start | bytes 12582916
  109.5 1.6 copy-start.18
  121.4 5.7 %copy-start.9 = (bf16[1,4096,512]{2,1,0:T(8,128)(2,1)S(1)}, bf16[1,4096,512]{2,1,0:T(8,128)(2,1)}, u32[]{:S(2)}) copy-start(bf16[1,4096,512]{2,1,0:T(8,128)(2,1)} %param.14) | copy-start | bytes 12582916
  130.4 5.0 %copy-start.3 = (bf16[1,2,256,4096]{3,2,1,0:T(8,128)(2,1)S(1)}, bf16[1,2,256,4096]{3,2,1,0:T(8,128)(2,1)}, u32[]{:S(2)}) copy-start(bf16[1,2,256,4096]{3,2,1,0:T(8,128)(2,1)} %param.8) | copy-start | bytes 12582916
  130.4 6.1 %copy-start.12 = (bf16[1,4096,512]{2,1,0:T(8,128)(2,1)S(1)}, bf16[1,4096,512]{2,1,0:T(8,128)(2,1)}, u32[]{:S(2)}) copy-start(bf16[1,4096,512]{2,1,0:T(8,128)(2,1)} %param.15) | copy-start | bytes 12582916
  130.4 7.3 %copy-start.14 = (f32[256,4096]{1,0:T(8,128)S(1)}, f32[256,4096]{1,0:T(8,128)}, u32[]{:S(2)}) copy-start(f32[256,4096]{1,0:T(8,128)} %fusion.59) | copy-start | bytes 12582916
  137.7 5.9 %copy-start.7 = (f32[256,4096]{1,0:T(8,128)}, f32[256,4096]{1,0:T(8,128)S(1)}, u32[]{:S(2)}) copy-start(f32[256,4096]{1,0:T(8,128)S(1)} %convolution_add_fusion.2) | copy-start | bytes 12582916
  151.9 56.8 %copy-start.4 = (f32[1,256,4096]{2,1,0:T(8,128)S(1)}, f32[1,256,4096]{2,1,0:T(8,128)}, u32[]{:S(2)}) copy-start(f32[1,256,4096]{2,1,0:T(8,128)} %get-tuple-element.12) | copy-start | bytes 12582916
  151.9 56.8 %copy-start.5 = (f32[1,256,4096]{2,1,0:T(8,128)S(1)}, f32[1,256,4096]{2,1,0:T(8,128)}, u32[]{:S(2)}) copy-start(f32[1,256,4096]{2,1,0:T(8,128)} %get-tuple-element.13) | copy-start | bytes 12582916
  151.9 56.8 %copy-start.6 = (bf16[2,256,4096]{2,1,0:T(8,128)(2,1)S(1)}, bf16[2,256,4096]{2,1,0:T(8,128)(2,1)}, u32[]{:S(2)}) copy-start(bf16[2,256,4096]{2,1,0:T(8,128)(2,1)} %all-gather.2.cloned.1.call-done) | copy-start | bytes 12582916
  157.4 51.3 %collective-permute-start = (bf16[2,256,4096]{2,1,0:T(8,128)(2,1)S(1)}, bf16[2,256,4096]{2,1,0:T(8,128)(2,1)S(1)}, u32[]{:S(2)}, u32[]{:S(2)}) collective-permute-start(bf16[2,256,4096]{2,1,0:T(8,128)(2,1)S(1)} %fusion.3), channel_id=1, source_target_pairs={{8,0},{16,8},{24,16},{9,1},{17,9},{25,17},{10,2},{18,10},{26,18},{... | collective-permute-start | bytes 12582920 | tf_op jit(solution)/shard_map/ppermute | solution.py:17
  210.8 55.0 %copy-start.21 = (u32[32]{0:T(128)S(1)}, u32[32]{0:T(128)}, u32[]{:S(2)}) copy-start(u32[32]{0:T(128)} %constant.43) | copy-start | bytes 388
  210.8 49.8 %collective-permute-start.1 = (bf16[2,256,4096]{2,1,0:T(8,128)(2,1)S(1)}, bf16[2,256,4096]{2,1,0:T(8,128)(2,1)S(1)}, u32[]{:S(2)}, u32[]{:S(2)}) collective-permute-start(bf16[2,256,4096]{2,1,0:T(8,128)(2,1)S(1)} %fusion.5), channel_id=1, source_target_pairs={{8,0},{16,8},{24,16},{9,1},{17,9},{25,17},{10,2},{18,10},{26,18},{... | collective-permute-start | bytes 12582920 | tf_op jit(solution)/shard_map/ppermute | solution.py:17
  263.9 141.4 %collective-permute-start.2 = (bf16[2,256,4096]{2,1,0:T(8,128)(2,1)}, bf16[2,256,4096]{2,1,0:T(8,128)(2,1)}, u32[]{:S(2)}, u32[]{:S(2)}) collective-permute-start(bf16[2,256,4096]{2,1,0:T(8,128)(2,1)} %fusion.7), channel_id=1, source_target_pairs={{8,0},{16,8},{24,16},{9,1},{17,9},{25,17},{10,2},{18,10},{26,18},{... | collective-permute-start | bytes 12582920 | tf_op jit(solution)/shard_map/ppermute | solution.py:17
Sparse Core Ops, SparseCore 0:
  10.4 36.9 all-gather.1
Sparse Core Ops, SparseCore 1:
  102.9 149.4 reduce-scatter.2
  256.3 146.6 reduce-scatter.4
where the time goes:
time: 428 us; the launch traced here: 422 us
  waiting for transfers between devices  198 us (46%)
  matrix products  87.9 us (21%)
  other arithmetic  48.2 us (11%)
  blocking collectives  32.4 us (8%)
  local copies, waits for them, and re-layouts  32.1 us (8%)
  between operations  16.8 us (4%)
  starting transfers between devices  6.48 us (2%)
    reduce_scatter x2, waiting for transfers between devices, shards(): shares = lax.psum_scatter(summed, 'dp', scatter_dimension=0, tiled=True)  100 us
    ppermute x3, waiting for transfers between devices, passed_along(): lax.ppermute(value, axis, [(source, source + steps) for source in range(f...  96.9 us
    unnamed x1, blocking collectives  32.4 us
    unnamed x53, local copies, waits for them, and re-layouts  24.7 us
    dot_general x2, matrix products, section_terms(): jnp.einsum('gjqk,qgjd->kgd', dscores, query_heads, preferred_element_type...  15.4 us
    broadcast_in_dim x3, other arithmetic, shards(): return (passed[None], key_share[None], value_share[None], gain_share[None])  13.7 us
    dot_general x2, matrix products, section_terms(): lax.dot_general(normed, dkeys, row_dims, preferred_element_type=jnp.float32)  12.8 us
    sub x2, other arithmetic, section_terms(): probs = jax.nn.softmax(scores, axis=-1)  11.5 us
  transfers between devices with their start and end apart: 6, of which 3 were waited for; matrix products, arithmetic and copies ran while one was open for 36% of the time, Pallas kernels for 0%

commit v1 on v0

v1 whole, which is shorter than its diff:
```python
import functools

import jax
import jax.numpy as jnp
from jax import lax
from jax.experimental import pallas as pl
from jax.experimental.pallas import tpu as pltpu
from jax.sharding import PartitionSpec as P

HD = 128
GRP = 8
EPS = 1e-05
PAD = 16
LOG2E = 1.4426950408889634
VMEM = 50 * 1024 * 1024
NT = (((1,), (1,)), ((), ()))
TN = (((0,), (0,)), ((), ()))


def attention_body(k_ref, v_ref, q_ref, g_ref, pos_ref, out_ref):
    length = k_ref.shape[0]
    scale = HD ** (-0.5)
    keys, values = k_ref[...], v_ref[...]
    key_at = lax.broadcasted_iota(jnp.int32, (length, length), 0)
    query_at = lax.broadcasted_iota(jnp.int32, (length, length), 1)
    distance = query_at - key_at
    allowed = (distance >= 0) & (distance <= pos_ref[0])
    dkeys = jnp.zeros((length, HD), jnp.float32)
    dvalues = jnp.zeros((length, HD), jnp.float32)
    for head in range(GRP):
        columns = slice(head * HD, (head + 1) * HD)
        query, grad = q_ref[0, :, columns], g_ref[0, :, columns]
        scores = lax.dot_general(keys, query, NT, preferred_element_type=jnp.float32)
        scores = jnp.where(allowed, scores, -1e30)
        top = jnp.max(scores, axis=0, keepdims=True)
        raw = jnp.exp2((scores - top) * (scale * LOG2E))
        probs = raw * (1.0 / jnp.sum(raw, axis=0, keepdims=True))
        dprobs = lax.dot_general(values, grad, NT, preferred_element_type=jnp.float32)
        total = jnp.sum(probs * dprobs, axis=0, keepdims=True)
        dscores = (probs * (dprobs - total)).astype(jnp.bfloat16)
        dkeys += jnp.dot(dscores, query, preferred_element_type=jnp.float32)
        dvalues += jnp.dot(probs.astype(jnp.bfloat16), grad, preferred_element_type=jnp.float32)
    out_ref[0] = (dkeys * scale).astype(jnp.bfloat16)
    out_ref[1] = dvalues.astype(jnp.bfloat16)


def attention_grads(keys, values, queries, grads, places, first, count):
    micro, length, _ = queries.shape
    wide = GRP * HD
    return pl.pallas_call(
        attention_body,
        grid=(count, micro),
        in_specs=[
            pl.BlockSpec((length, HD), lambda g, m: (m, first + g)),
            pl.BlockSpec((length, HD), lambda g, m: (m, first + g)),
            pl.BlockSpec((1, length, wide), lambda g, m: (m, 0, first + g)),
            pl.BlockSpec((1, length, wide), lambda g, m: (m, 0, first + g)),
            pl.BlockSpec((1, 1, length), lambda g, m: (m, 0, 0)),
        ],
        out_specs=pl.BlockSpec((2, length, HD), lambda g, m: (0, m, g)),
        out_shape=jax.ShapeDtypeStruct((2, micro * length, count * HD), jnp.bfloat16),
        cost_estimate=pl.CostEstimate(
            flops=8 * count * micro * GRP * length * length * HD,
            bytes_accessed=4 * count * micro * length * wide,
            transcendentals=count * micro * GRP * length * length,
        ),
        compiler_params=pltpu.CompilerParams(vmem_limit_bytes=VMEM),
        name="attention_grads",
    )(keys, values, queries, grads, places)


def weight_body(own_ref, other_ref, own_d_ref, other_d_ref, out_ref):
    rows = own_ref.shape[1]
    own_d = jnp.concatenate([own_d_ref[0], own_d_ref[1]], axis=1)
    other_d = jnp.concatenate([other_d_ref[0], other_d_ref[1]], axis=1)
    total = lax.dot_general(own_ref[...], own_d, TN, preferred_element_type=jnp.float32)
    total += lax.dot_general(other_ref[...], other_d, TN, preferred_element_type=jnp.float32)
    most = jnp.maximum(jnp.max(jnp.abs(total), axis=0, keepdims=True), 1e-30)
    power = jnp.ceil(jnp.log2(most * (1.0 / 32000.0)))
    coded = jnp.round(total * jnp.exp2(-power)).astype(jnp.int32)
    out_ref[0, :rows] = coded.astype(jnp.int16)
    tail = jnp.broadcast_to(power.astype(jnp.int32), (PAD, power.shape[1]))
    out_ref[0, rows:] = tail.astype(jnp.int16)


def weight_terms(own, other, own_d, other_d, chunks):
    tokens, width = own.shape
    rows = width // chunks
    columns = 2 * own_d.shape[2]
    block = pl.BlockSpec((tokens, rows), lambda k: (0, k))
    whole = pl.BlockSpec(own_d.shape, lambda k: (0, 0, 0))
    return pl.pallas_call(
        weight_body,
        grid=(chunks,),
        in_specs=[block, block, whole, whole],
        out_specs=pl.BlockSpec((1, rows + PAD, columns), lambda k: (k, 0, 0)),
        out_shape=jax.ShapeDtypeStruct((chunks, rows + PAD, columns), jnp.int16),
        cost_estimate=pl.CostEstimate(
            flops=4 * tokens * width * columns,
            bytes_accessed=4 * tokens * width + 2 * width * columns,
            transcendentals=0,
        ),
        compiler_params=pltpu.CompilerParams(vmem_limit_bytes=VMEM),
        name="weight_terms",
    )(own, other, own_d, other_d)


def branch_body(x_ref, low_ref, high_ref, wk_ref, wv_ref, gain_ref, out_ref, term_ref):
    width = x_ref.shape[1]
    dk = jnp.concatenate([low_ref[0], high_ref[0]], axis=1)
    dv = jnp.concatenate([low_ref[1], high_ref[1]], axis=1)
    dnormed = lax.dot_general(dk, wk_ref[...], NT, preferred_element_type=jnp.float32)
    dnormed += lax.dot_general(dv, wv_ref[...], NT, preferred_element_type=jnp.float32)
    x = x_ref[...].astype(jnp.float32)
    inverse = lax.rsqrt(jnp.sum(x * x, axis=-1, keepdims=True) * (1.0 / width) + EPS)
    unit = x * inverse
    product = dnormed * unit
    term = jnp.sum(product, axis=0, keepdims=True)
    first = pl.program_id(0) == 0

    @pl.when(first)
    def _():
        term_ref[...] = term

    @pl.when(jnp.logical_not(first))
    def _():
        term_ref[...] += term

    gain = gain_ref[...]
    mean = jnp.sum(product * gain, axis=-1, keepdims=True) * (1.0 / width)
    out_ref[...] = inverse * (dnormed * gain - unit * mean)


def branch_terms(x, low, high, wk, wv, gain):
    tokens, width = x.shape
    rows = 128
    half = low.shape[2]
    weight = pl.BlockSpec(wk.shape, lambda i: (0, 0))
    return pl.pallas_call(
        branch_body,
        grid=(tokens // rows,),
        in_specs=[
            pl.BlockSpec((rows, width), lambda i: (i, 0)),
            pl.BlockSpec((2, rows, half), lambda i: (0, i, 0)),
            pl.BlockSpec((2, rows, half), lambda i: (0, i, 0)),
            weight,
            weight,
            pl.BlockSpec((1, width), lambda i: (0, 0)),
        ],
        out_specs=[
            pl.BlockSpec((rows, width), lambda i: (i, 0)),
            pl.BlockSpec((1, width), lambda i: (0, 0)),
        ],
        out_shape=[
            jax.ShapeDtypeStruct((tokens, width), jnp.float32),
            jax.ShapeDtypeStruct((1, width), jnp.float32),
        ],
        cost_estimate=pl.CostEstimate(
            flops=4 * tokens * width * wk.shape[1],
            bytes_accessed=6 * tokens * width + 4 * width * wk.shape[1],
            transcendentals=0,
        ),
        compiler_params=pltpu.CompilerParams(vmem_limit_bytes=VMEM),
        name="branch_terms",
    )(x, low, high, wk, wv, gain)


def shards(
    layer_input, queries, attn_grad, top_grad, positions, norm_gain, key_weight, value_weight
):
    _, micro, length, width = layer_input.shape
    tokens = micro * length
    replicas = lax.axis_size("dp")
    chunks = replicas // 2
    rows = width // replicas
    seq_total = micro * replicas
    me = lax.axis_index("dp")
    side = lax.rem(me, 2)
    place = me // 2
    swap = [(i, i ^ 1) for i in range(replicas)]
    wk, wv = key_weight[0], value_weight[0]
    x = layer_input[0].reshape(tokens, width)
    top_full = lax.all_gather(top_grad, "section", axis=2, tiled=True)

    def parity(values, which):
        parts = []
        for k in range(chunks):
            owner = lax.rem(place + k, chunks) * 2 + which
            parts.append(lax.dynamic_slice_in_dim(values, owner * rows, rows, values.ndim - 1))
        return jnp.concatenate(parts, axis=-1)

    x_f = x.astype(jnp.float32)
    inverse = lax.rsqrt(jnp.mean(x_f * x_f, axis=-1, keepdims=True) + EPS)
    normed = (x_f * inverse * norm_gain).astype(jnp.bfloat16)
    other = lax.ppermute(parity(normed, 1 - side), "dp", swap)
    own = parity(normed, side)
    keys = jnp.dot(normed, wk, preferred_element_type=jnp.float32).astype(jnp.bfloat16)
    values = jnp.dot(normed, wv, preferred_element_type=jnp.float32).astype(jnp.bfloat16)

    heads = keys.shape[1] // HD
    half = heads // 2
    places = positions.reshape(micro, 1, length)
    grads, sums = [], []

    def shift_from(k):
        pairs = []
        for i in range(replicas):
            target = ((i // 2 + k) % chunks) * 2 + i % 2
            pairs.append((i, target))
        return pairs

    for first in (0, half):
        mine = attention_grads(keys, values, queries[0], attn_grad[0], places, first, half)
        grads.append(mine)
        theirs = lax.ppermute(mine, "dp", swap)
        coded = weight_terms(own, other, mine, theirs, chunks)
        pieces = [coded[0]]
        for k in range(1, chunks):
            pieces.append(lax.ppermute(coded[k], "dp", shift_from(k)))
        sums.append(pieces)

    branch, term = branch_terms(x, grads[0], grads[1], wk, wv, norm_gain)

    gain_part = parity(term, side) + lax.ppermute(parity(term, 1 - side), "dp", swap)
    gain_share = gain_part[:, :rows]
    for k in range(1, chunks):
        piece = gain_part[:, k * rows : (k + 1) * rows]
        gain_share = gain_share + lax.ppermute(piece, "dp", shift_from(k))
    gain_share = gain_share / seq_total

    sections = lax.axis_size("section")
    section = lax.axis_index("section")
    passed = []
    for m in range(micro):
        mine = branch[m * length : (m + 1) * length]
        current = (top_full[m].astype(jnp.float32) + mine).astype(jnp.bfloat16)
        for s in range(sections - 2, -1, -1):
            came = lax.ppermute(current, "section", [(s + 1, s)])
            added = (came.astype(jnp.float32) + mine).astype(jnp.bfloat16)
            current = jnp.where(section == s, added, current)
        passed.append(current)
    passed = jnp.stack(passed)

    def decoded(pieces):
        total = None
        for piece in pieces:
            unit = jnp.exp2(piece[rows : rows + 1].astype(jnp.float32))
            part = piece[:rows].astype(jnp.float32) * unit
            total = part if total is None else total + part
        return total / seq_total

    low, high = decoded(sums[0]), decoded(sums[1])
    wide = half * HD
    key_share = jnp.concatenate([low[:, :wide], high[:, :wide]], axis=1)
    value_share = jnp.concatenate([low[:, wide:], high[:, wide:]], axis=1)
    return (passed[None], key_share[None], value_share[None], gain_share)


def solution(mesh):
    return jax.shard_map(
        shards,
        mesh=mesh,
        in_specs=(
            P("section", None, "dp", None),
            P("section", None, "dp", None),
            P("section", None, "dp", None),
            P(None, "dp", "section"),
            P(None, "dp"),
            P("section", None),
            P("section", None, None),
            P("section", None, None),
        ),
        out_specs=(
            P("section", None, "dp", None),
            P("section", "dp", None),
            P("section", "dp", None),
            P("section", "dp"),
        ),
        check_vma=False,
    )
```

time: 428 us -> 259 us (0.61); the launches traced: 422 us -> 259 us
  waiting for transfers between devices: 198 us -> 98.2 us
  matrix products: 87.9 us -> 4.72 us
  Pallas kernels: 0 us -> 58.7 us
  blocking collectives: 32.4 us -> 0 us
  local copies, waits for them, and re-layouts: 32.1 us -> 6.39 us
  starting transfers between devices: 6.48 us -> 25.5 us
    reduce_scatter x2 -> x0, waiting for transfers between devices: 100 us -> none  [shards(): shares = lax.psum_scatter(summed, 'dp', scatter_dimension=0, tiled=True)]
    dot_general x20 -> x2, matrix products: 87.9 us -> 4.72 us  [the longest x1 2.36 us: shards(): jnp.dot(normed, wv, preferred_element_type=jnp.float32).astype(jnp.bfloat16)]
    pallas_call x0 -> x5, Pallas kernels: none -> 58.7 us  [the longest x2 26.6 us: attention_grads(): pl.pallas_call(attention_body, grid=(count, micro), in_specs=[pl.BlockSpe...]
    unnamed x1 -> x0, blocking collectives: 32.4 us -> none
    unnamed x53 -> x19, local copies, waits for them, and re-layouts: 24.7 us -> 1.08 us
    ppermute x3 -> x19, starting transfers between devices: 6.15 us -> 25.4 us  [the longest x6 10.8 us: shards(): came = lax.ppermute(current, 'section', [(s + 1, s)])]
    select_n x0 -> x3, other arithmetic: none -> 13.4 us  [shards(): current = jnp.where(section == s, added, current)]
    sub x2 -> x0, other arithmetic: 11.5 us -> none  [section_terms(): probs = jax.nn.softmax(scores, axis=-1)]
  transfers between devices with their start and end apart: 6 -> 20, of which waited for: 3 -> 5; matrix products, arithmetic and copies ran while one was open for 36% -> 17% of each run, Pallas kernels for 0% -> 23%
where the time goes in v1:
time: 259 us
  waiting for transfers between devices  98.2 us (38%)
  Pallas kernels  58.7 us (23%)
  other arithmetic  50.9 us (20%)
  starting transfers between devices  25.5 us (10%)
  between operations  14.4 us (6%)
  local copies, waits for them, and re-layouts  6.39 us (2%)
  matrix products  4.72 us (2%)
    ppermute x6, waiting for transfers between devices, shards(): pieces.append(lax.ppermute(coded[k], 'dp', shift_from(k)))  56.7 us
    pallas_call x2, Pallas kernels, attention_grads(): pl.pallas_call(attention_body, grid=(count, micro), in_specs=[pl.BlockSpe...  26.6 us
    ppermute x6, waiting for transfers between devices, shards(): came = lax.ppermute(current, 'section', [(s + 1, s)])  26.3 us
    pallas_call x1, Pallas kernels, branch_terms(): pl.pallas_call(branch_body, grid=(tokens // rows,), in_specs=[pl.BlockSpe...  19.9 us
    ppermute x1, waiting for transfers between devices, shards(): other = lax.ppermute(parity(normed, 1 - side), 'dp', swap)  14.5 us
    select_n x3, other arithmetic, shards(): current = jnp.where(section == s, added, current)  13.4 us
    pallas_call x2, Pallas kernels, weight_terms(): pl.pallas_call(weight_body, grid=(chunks,), in_specs=[block, block, whole...  12.2 us
    ppermute x6, starting transfers between devices, shards(): came = lax.ppermute(current, 'section', [(s + 1, s)])  10.8 us
  transfers between devices with their start and end apart: 20, of which 5 were waited for; matrix products, arithmetic and copies ran while one was open for 17% of the time, Pallas kernels for 23%

profile of v1, /device:TPU:1, one launch (start us, length us, event | category | flops | bytes accessed | tf_op | source)
XLA Modules:
  0.0 258.7 jit_solution(11193991363631922720)
XLA Ops:
  7.2 0.7 all-gather.2.cloned.1.call-update
  7.9 0.8 reshape.96.pos_ref
  8.8 3.3 %fusion = f32[2,256]{1,0:T(2,128)S(1)} fusion(bf16[1,2,256,4096]{3,2,1,0:T(8,128)(2,1)} %param.8), kind=kLoop, calls=%fused_computation.2 | loop fusion | flops 6290944 | bytes 4196352 | tf_op jit(solution)/shard_map/reduce_sum | solution.py:193
  12.1 1.7 fusion.2
  14.2 2.4 convolution_convert_fusion.1.k_ref
  16.6 2.4 convolution_convert_fusion.v_ref
  19.0 13.5 %attention_grads.2.low_ref.own_d_ref = bf16[2,512,256]{2,1,0:T(8,128)(2,1)S(1)} custom-call(bf16[512,512]{1,0:T(8,128)(2,1)S(1)} %convolution_convert_fusion.1.k_ref, bf16[512,512]{1,0:T(8,128)(2,1)S(1)} %convolution_convert_fusion.v_ref, bf16[2,256,4096]{2,1,0:T(8,128)(2,1)} %bitcast.72, bf16[2,256,4096]{2,1,0:T(8,128)(2,1)} %bitcast.74, ...), custom_call_target="tpu_custom_call" | custom-call | flops 2147483648 | bytes 4194304 | tf_op jit(solution)/shard_map/attention_grads/pallas_call | solution.py:50
  32.4 13.2 %attention_grads.3.high_ref.own_d_ref = bf16[2,512,256]{2,1,0:T(8,128)(2,1)S(1)} custom-call(bf16[512,512]{1,0:T(8,128)(2,1)S(1)} %convolution_convert_fusion.1.k_ref, bf16[512,512]{1,0:T(8,128)(2,1)S(1)} %convolution_convert_fusion.v_ref, bf16[2,256,4096]{2,1,0:T(8,128)(2,1)} %bitcast.73, bf16[2,256,4096]{2,1,0:T(8,128)(2,1)} %bitcast.75, ...), custom_call_target="tpu_custom_call" | custom-call | flops 2147483648 | bytes 4194304 | tf_op jit(solution)/shard_map/attention_grads/pallas_call | solution.py:50
  45.6 19.9 %branch_terms.1 = (f32[512,4096]{1,0:T(8,128)}, f32[1,4096]{1,0:T(1,128)S(1)}) custom-call(bf16[512,4096]{1,0:T(8,128)(2,1)} %bitcast.71, bf16[2,512,256]{2,1,0:T(8,128)(2,1)S(1)} %attention_grads.2.low_ref.own_d_ref, bf16[2,512,256]{2,1,0:T(8,128)(2,1)S(1)} %attention_grads.3.high_ref.own_d_ref, bf16[4096,512]{1,0:T(8,128)(2,1)} %bitcast.87, ...), custom_call_target="tpu_custom_call" | custom-call | flops 4294967296 | bytes 20971520 | tf_op jit(solution)/shard_map/branch_terms/pallas_call | solution.py:139
  65.5 7.2 %fusion.4 = (bf16[256,4096]{1,0:T(8,128)(2,1)}, bf16[256,4096]{1,0:T(8,128)(2,1)}) fusion(f32[512,4096]{1,0:T(8,128)} %get-tuple-element.6, bf16[2,256,4096]{2,1,0:T(8,128)(2,1)} %all-gather.2.cloned.1.call-done), kind=kLoop, calls=%fused_computation.10 | loop fusion | flops 6291456 | bytes 16777216 | tf_op jit(solution)/shard_map/convert_element_type | solution.py:236
  72.7 2.0 collective-permute-start
  74.8 5.8 %fusion.5 = bf16[256,4096]{1,0:T(8,128)(2,1)} fusion(bf16[256,4096]{1,0:T(8,128)(2,1)} %get-tuple-element.8, f32[512,4096]{1,0:T(8,128)} %get-tuple-element.6, bf16[256,4096]{1,0:T(8,128)(2,1)} %collective-permute-done, pred[]{:T(512)S(6)} %eq.14), kind=kLoop, calls=%fused_computation.17 | loop fusion | flops 4194304 | bytes 10485761 | tf_op jit(solution)/shard_map/jit(_where)/select_n | solution.py:240
  80.5 1.3 collective-permute-start.1
  81.8 2.1 collective-permute-start.11
  84.2 2.2 collective-permute-start.3
  86.3 26.3 %collective-permute-done.1 = bf16[256,4096]{1,0:T(8,128)(2,1)} collective-permute-done((bf16[256,4096]{1,0:T(8,128)(2,1)}, bf16[256,4096]{1,0:T(8,128)(2,1)}, u32[]{:S(2)}, u32[]{:S(2)}) %collective-permute-start.1) | collective-permute-done | bytes 2097184 | tf_op jit(solution)/shard_map/ppermute | solution.py:238
  112.6 5.2 %fusion.6 = bf16[256,4096]{1,0:T(8,128)(2,1)} fusion(bf16[256,4096]{1,0:T(8,128)(2,1)} %fusion.5, f32[512,4096]{1,0:T(8,128)} %get-tuple-element.6, bf16[256,4096]{1,0:T(8,128)(2,1)} %collective-permute-done.1, pred[]{:T(512)S(6)} %eq.13), kind=kLoop, calls=%fused_computation.18 | loop fusion | flops 4194304 | bytes 10485761 | tf_op jit(solution)/shard_map/jit(_where)/select_n | solution.py:240
  117.8 2.7 %collective-permute-start.2 = (bf16[256,4096]{1,0:T(8,128)(2,1)}, bf16[256,4096]{1,0:T(8,128)(2,1)}, u32[]{:S(2)}, u32[]{:S(2)}) collective-permute-start(bf16[256,4096]{1,0:T(8,128)(2,1)} %fusion.6), channel_id=1, source_target_pairs={{8,0},{9,1},{10,2},{11,3},{12,4},{13,5},{14,6},{15,7}} | collective-permute-start | bytes 6291464 | tf_op jit(solution)/shard_map/ppermute | solution.py:238
  120.4 1.9 multiply_convert_fusion
  122.3 1.3 constant_dynamic-slice_fusion.11
  123.6 1.6 pad_maximum_fusion.1
  125.2 1.3 collective-permute-start.6
  126.6 3.5 %collective-permute-start.18 = (f32[1,512]{1,0:T(1,128)S(1)}, f32[1,512]{1,0:T(1,128)S(1)}, u32[]{:S(2)}, u32[]{:S(2)}) collective-permute-start(f32[1,512]{1,0:T(1,128)S(1)} %get-tuple-element.39), channel_id=1, source_target_pairs={{0,6},{1,7},{2,0},{3,1},{4,2},{5,3},{6,4},{7,5},{8,14},{9,15},{10,... | collective-permute-start | bytes 6152 | tf_op jit(solution)/shard_map/ppermute | solution.py:228
  130.5 8.9 %fusion.8 = (bf16[1,256,4096]{2,1,0:T(8,128)(2,1)}, bf16[256,4096]{1,0:T(8,128)(2,1)}) fusion(bf16[256,4096]{1,0:T(8,128)(2,1)} %fusion.6, f32[512,4096]{1,0:T(8,128)} %get-tuple-element.6, bf16[256,4096]{1,0:T(8,128)(2,1)} %collective-permute-done.2, pred[]{:T(512)S(6)} %eq.12, bf16[256,4096]{1,0:T(8,128)(2,1)} %get-tuple-element.9, ...), kind=kLoop, calls=%fused_computation.20 | loop fusion | flops 8388608 | bytes 20971522 | tf_op jit(solution)/shard_map/stack | solution.py:242
  139.3 1.3 collective-permute-start.4
  141.3 0.6 fusion.39
  141.8 14.5 %collective-permute-done.6.other_ref = bf16[512,2048]{1,0:T(8,128)(2,1)} collective-permute-done((bf16[512,2048]{1,0:T(8,128)(2,1)}, bf16[512,2048]{1,0:T(8,128)(2,1)}, u32[]{:S(2)}, u32[]{:S(2)}) %collective-permute-start.6) | collective-permute-done | bytes 2097184 | tf_op jit(solution)/shard_map/ppermute | solution.py:195
  156.4 6.1 %weight_terms.3 = s16[4,528,512]{2,1,0:T(8,128)(2,1)} custom-call(bf16[512,2048]{1,0:T(8,128)(2,1)S(1)} %pad_maximum_fusion.own_ref, bf16[512,2048]{1,0:T(8,128)(2,1)} %collective-permute-done.6.other_ref, bf16[2,512,256]{2,1,0:T(8,128)(2,1)S(1)} %attention_grads.3.high_ref.own_d_ref, bf16[2,512,256]{2,1,0:T(8,128)(2,1)S(1)} %collective-permute-done.11.other_d_ref), custom_call_target="tpu_custom_call" | custom-call | flops 2147483648 | bytes 6291456 | tf_op jit(solution)/shard_map/weight_terms/pallas_call | solution.py:92
  162.5 1.5 slice_bitcast_fusion.4
  164.0 3.5 %collective-permute-start.14 = (s16[528,512]{1,0:T(8,128)(2,1)S(1)}, s16[528,512]{1,0:T(8,128)(2,1)S(1)}, u32[]{:S(2)}, u32[]{:S(2)}) collective-permute-start(s16[528,512]{1,0:T(8,128)(2,1)S(1)} %get-tuple-element.24), channel_id=1, source_target_pairs={{0,6},{1,7},{2,0},{3,1},{4,2},{5,3},{6,4},{7,5},{8,14},{9,15},{10,... | collective-permute-start | bytes 1622024 | tf_op jit(solution)/shard_map/ppermute | solution.py:219
  167.9 0.7 fusion.30
  168.7 6.1 %weight_terms.2 = s16[4,528,512]{2,1,0:T(8,128)(2,1)} custom-call(bf16[512,2048]{1,0:T(8,128)(2,1)S(1)} %pad_maximum_fusion.own_ref, bf16[512,2048]{1,0:T(8,128)(2,1)} %collective-permute-done.6.other_ref, bf16[2,512,256]{2,1,0:T(8,128)(2,1)S(1)} %attention_grads.2.low_ref.own_d_ref, bf16[2,512,256]{2,1,0:T(8,128)(2,1)S(1)} %collective-permute-done.7.other_d_ref), custom_call_target="tpu_custom_call" | custom-call | flops 2147483648 | bytes 6291456 | tf_op jit(solution)/shard_map/weight_terms/pallas_call | solution.py:92
  174.8 1.5 slice_bitcast_fusion.7
  176.3 2.9 %collective-permute-start.10 = (s16[528,512]{1,0:T(8,128)(2,1)S(1)}, s16[528,512]{1,0:T(8,128)(2,1)S(1)}, u32[]{:S(2)}, u32[]{:S(2)}) collective-permute-start(s16[528,512]{1,0:T(8,128)(2,1)S(1)} %get-tuple-element.21), channel_id=1, source_target_pairs={{0,6},{1,7},{2,0},{3,1},{4,2},{5,3},{6,4},{7,5},{8,14},{9,15},{10,... | collective-permute-start | bytes 1622024 | tf_op jit(solution)/shard_map/ppermute | solution.py:219
  179.1 0.7 fusion.38
  179.8 3.4 %collective-permute-done.14 = s16[528,512]{1,0:T(8,128)(2,1)S(1)} collective-permute-done((s16[528,512]{1,0:T(8,128)(2,1)S(1)}, s16[528,512]{1,0:T(8,128)(2,1)S(1)}, u32[]{:S(2)}, u32[]{:S(2)}) %collective-permute-start.14) | collective-permute-done | bytes 540704 | tf_op jit(solution)/shard_map/ppermute | solution.py:219
  183.3 37.0 %collective-permute-done.13 = s16[528,512]{1,0:T(8,128)(2,1)} collective-permute-done((s16[528,512]{1,0:T(8,128)(2,1)S(1)}, s16[528,512]{1,0:T(8,128)(2,1)}, u32[]{:S(2)}, u32[]{:S(2)}) %collective-permute-start.13) | collective-permute-done | bytes 540704 | tf_op jit(solution)/shard_map/ppermute | solution.py:219
  220.3 0.7 fusion.26
  221.0 2.5 fusion.10
  223.5 1.4 collective-permute-start.5
  225.0 0.7 fusion.28
  225.7 16.2 %collective-permute-done.9 = s16[528,512]{1,0:T(8,128)(2,1)S(1)} collective-permute-done((s16[528,512]{1,0:T(8,128)(2,1)S(1)}, s16[528,512]{1,0:T(8,128)(2,1)S(1)}, u32[]{:S(2)}, u32[]{:S(2)}) %collective-permute-start.9) | collective-permute-done | bytes 540704 | tf_op jit(solution)/shard_map/ppermute | solution.py:219
  242.0 2.2 fusion.16
  244.3 1.9 fusion.20
  246.2 1.6 maximum_bitcast_fusion.1
  247.8 1.0 fusion.12
  248.9 0.5 copy-done.3
  249.4 2.4 maximum_bitcast_fusion
  (55 shorter events, 2.6 us)
Async XLA Ops:
  7.2 4.9 %copy-start = (f32[1,4096]{1,0:T(1,128)S(1)}, f32[1,4096]{1,0:T(1,128)}, u32[]{:S(2)}) copy-start(f32[1,4096]{1,0:T(1,128)} %gain_ref.1) | copy-start | bytes 49156
  7.2 58.3 %all-gather.2.cloned.1.call-start = ((), (), s32[]{:S(2)}) async-start(), calls=%async_computation | async-start | bytes 5242880 | tf_op jit(solution)/shard_map/all_gather | solution.py:183
  7.9 4.1 %copy-start.1 = (bf16[1,2,256,4096]{3,2,1,0:T(8,128)(2,1)S(1)}, bf16[1,2,256,4096]{3,2,1,0:T(8,128)(2,1)}, u32[]{:S(2)}) copy-start(bf16[1,2,256,4096]{3,2,1,0:T(8,128)(2,1)} %param.8) | copy-start | bytes 12582916
  12.1 2.2 copy-start.5
  14.2 2.4 copy-start.6
  72.7 2.0 collective-permute-start
  80.5 32.0 %collective-permute-start.1 = (bf16[256,4096]{1,0:T(8,128)(2,1)}, bf16[256,4096]{1,0:T(8,128)(2,1)}, u32[]{:S(2)}, u32[]{:S(2)}) collective-permute-start(bf16[256,4096]{1,0:T(8,128)(2,1)} %fusion.5), channel_id=1, source_target_pairs={{16,8},{17,9},{18,10},{19,11},{20,12},{21,13},{22,14},{23,15}} | collective-permute-start | bytes 6291464 | tf_op jit(solution)/shard_map/ppermute | solution.py:238
  81.8 60.0 %collective-permute-start.11 = (bf16[2,512,256]{2,1,0:T(8,128)(2,1)S(1)}, bf16[2,512,256]{2,1,0:T(8,128)(2,1)S(1)}, u32[]{:S(2)}, u32[]{:S(2)}) collective-permute-start(bf16[2,512,256]{2,1,0:T(8,128)(2,1)S(1)} %attention_grads.3.high_ref.own_d_ref), channel_id=1, source_target_pairs={{0,1},{1,0},{2,3},{3,2},{4,5},{5,4},{6,7},{7,6},{8,9},{9,8},{10,11... | collective-permute-start | bytes 1572872 | tf_op jit(solution)/shard_map/ppermute | solution.py:215
  84.0 42.6 %collective-permute-start.15 = (f32[1,2048]{1,0:T(1,128)S(1)}, f32[1,2048]{1,0:T(1,128)S(1)}, u32[]{:S(2)}, u32[]{:S(2)}) collective-permute-start(f32[1,2048]{1,0:T(1,128)S(1)} %pad_maximum_fusion.2), channel_id=1, source_target_pairs={{0,1},{1,0},{2,3},{3,2},{4,5},{5,4},{6,7},{7,6},{8,9},{9,8},{10,11... | collective-permute-start | bytes 24584 | tf_op jit(solution)/shard_map/ppermute | solution.py:224
  84.2 36.3 %copy-start.2 = (bf16[1,2,256,4096]{3,2,1,0:T(8,128)(2,1)S(1)}, bf16[1,2,256,4096]{3,2,1,0:T(8,128)(2,1)}, u32[]{:S(2)}) copy-start(bf16[1,2,256,4096]{3,2,1,0:T(8,128)(2,1)} %param.8) | copy-start | bytes 12582916
  84.2 45.9 %collective-permute-start.3 = (bf16[256,4096]{1,0:T(8,128)(2,1)}, bf16[256,4096]{1,0:T(8,128)(2,1)}, u32[]{:S(2)}, u32[]{:S(2)}) collective-permute-start(bf16[256,4096]{1,0:T(8,128)(2,1)} %get-tuple-element.9), channel_id=1, source_target_pairs={{24,16},{25,17},{26,18},{27,19},{28,20},{29,21},{30,22},{31,23}} | collective-permute-start | bytes 6291464 | tf_op jit(solution)/shard_map/ppermute | solution.py:238
  117.8 12.3 %collective-permute-start.2 = (bf16[256,4096]{1,0:T(8,128)(2,1)}, bf16[256,4096]{1,0:T(8,128)(2,1)}, u32[]{:S(2)}, u32[]{:S(2)}) collective-permute-start(bf16[256,4096]{1,0:T(8,128)(2,1)} %fusion.6), channel_id=1, source_target_pairs={{8,0},{9,1},{10,2},{11,3},{12,4},{13,5},{14,6},{15,7}} | collective-permute-start | bytes 6291464 | tf_op jit(solution)/shard_map/ppermute | solution.py:238
  125.2 31.1 %collective-permute-start.6 = (bf16[512,2048]{1,0:T(8,128)(2,1)}, bf16[512,2048]{1,0:T(8,128)(2,1)}, u32[]{:S(2)}, u32[]{:S(2)}) collective-permute-start(bf16[512,2048]{1,0:T(8,128)(2,1)} %pad_maximum_fusion.1), channel_id=1, source_target_pairs={{0,1},{1,0},{2,3},{3,2},{4,5},{5,4},{6,7},{7,6},{8,9},{9,8},{10,11... | collective-permute-start | bytes 6291464 | tf_op jit(solution)/shard_map/ppermute | solution.py:195
  126.6 12.8 %collective-permute-start.18 = (f32[1,512]{1,0:T(1,128)S(1)}, f32[1,512]{1,0:T(1,128)S(1)}, u32[]{:S(2)}, u32[]{:S(2)}) collective-permute-start(f32[1,512]{1,0:T(1,128)S(1)} %get-tuple-element.39), channel_id=1, source_target_pairs={{0,6},{1,7},{2,0},{3,1},{4,2},{5,3},{6,4},{7,5},{8,14},{9,15},{10,... | collective-permute-start | bytes 6152 | tf_op jit(solution)/shard_map/ppermute | solution.py:228
  130.0 10.9 %collective-permute-start.17 = (f32[1,512]{1,0:T(1,128)S(1)}, f32[1,512]{1,0:T(1,128)S(1)}, u32[]{:S(2)}, u32[]{:S(2)}) collective-permute-start(f32[1,512]{1,0:T(1,128)S(1)} %get-tuple-element.40), channel_id=1, source_target_pairs={{0,4},{1,5},{2,6},{3,7},{4,0},{5,1},{6,2},{7,3},{8,12},{9,13},{10,... | collective-permute-start | bytes 6152 | tf_op jit(solution)/shard_map/ppermute | solution.py:228
  130.0 10.6 %copy-start.4 = (bf16[512,512]{1,0:T(8,128)(2,1)S(1)}, bf16[512,512]{1,0:T(8,128)(2,1)}, u32[]{:S(2)}) copy-start(bf16[512,512]{1,0:T(8,128)(2,1)} %get-tuple-element.19) | copy-start | bytes 1572868
  130.0 11.2 %collective-permute-start.16 = (f32[1,512]{1,0:T(1,128)S(1)}, f32[1,512]{1,0:T(1,128)S(1)}, u32[]{:S(2)}, u32[]{:S(2)}) collective-permute-start(f32[1,512]{1,0:T(1,128)S(1)} %get-tuple-element.38), channel_id=1, source_target_pairs={{0,2},{1,3},{2,4},{3,5},{4,6},{5,7},{6,0},{7,1},{8,10},{9,11},{10,... | collective-permute-start | bytes 6152 | tf_op jit(solution)/shard_map/ppermute | solution.py:228
  139.3 81.7 %collective-permute-start.4 = (bf16[256,4096]{1,0:T(8,128)(2,1)}, bf16[256,4096]{1,0:T(8,128)(2,1)}, u32[]{:S(2)}, u32[]{:S(2)}) collective-permute-start(bf16[256,4096]{1,0:T(8,128)(2,1)} %get-tuple-element.11), channel_id=1, source_target_pairs={{16,8},{17,9},{18,10},{19,11},{20,12},{21,13},{22,14},{23,15}} | collective-permute-start | bytes 6291464 | tf_op jit(solution)/shard_map/ppermute | solution.py:238
  141.0 27.7 %collective-permute-start.7 = (bf16[2,512,256]{2,1,0:T(8,128)(2,1)S(1)}, bf16[2,512,256]{2,1,0:T(8,128)(2,1)S(1)}, u32[]{:S(2)}, u32[]{:S(2)}) collective-permute-start(bf16[2,512,256]{2,1,0:T(8,128)(2,1)S(1)} %attention_grads.2.low_ref.own_d_ref), channel_id=1, source_target_pairs={{0,1},{1,0},{2,3},{3,2},{4,5},{5,4},{6,7},{7,6},{8,9},{9,8},{10,11... | collective-permute-start | bytes 1572872 | tf_op jit(solution)/shard_map/ppermute | solution.py:215
  156.4 64.6 %slice-start = ((s8[8388608]{0:T(1024)(128)(4,1)}), s8[4194304]{0:T(1024)(128)(4,1)S(1)}, s32[]{:S(2)}) async-start(s8[8388608]{0:T(1024)(128)(4,1)} %bitcast.69), calls=%async_computation.1 | async-start | bytes 8388608
  164.0 19.3 %collective-permute-start.14 = (s16[528,512]{1,0:T(8,128)(2,1)S(1)}, s16[528,512]{1,0:T(8,128)(2,1)S(1)}, u32[]{:S(2)}, u32[]{:S(2)}) collective-permute-start(s16[528,512]{1,0:T(8,128)(2,1)S(1)} %get-tuple-element.24), channel_id=1, source_target_pairs={{0,6},{1,7},{2,0},{3,1},{4,2},{5,3},{6,4},{7,5},{8,14},{9,15},{10,... | collective-permute-start | bytes 1622024 | tf_op jit(solution)/shard_map/ppermute | solution.py:219
  167.5 52.8 %collective-permute-start.13 = (s16[528,512]{1,0:T(8,128)(2,1)S(1)}, s16[528,512]{1,0:T(8,128)(2,1)}, u32[]{:S(2)}, u32[]{:S(2)}) collective-permute-start(s16[528,512]{1,0:T(8,128)(2,1)S(1)} %get-tuple-element.25), channel_id=1, source_target_pairs={{0,4},{1,5},{2,6},{3,7},{4,0},{5,1},{6,2},{7,3},{8,12},{9,13},{10,... | collective-permute-start | bytes 1622024 | tf_op jit(solution)/shard_map/ppermute | solution.py:219
  167.5 57.5 %collective-permute-start.12 = (s16[528,512]{1,0:T(8,128)(2,1)S(1)}, s16[528,512]{1,0:T(8,128)(2,1)}, u32[]{:S(2)}, u32[]{:S(2)}) collective-permute-start(s16[528,512]{1,0:T(8,128)(2,1)S(1)} %get-tuple-element.23), channel_id=1, source_target_pairs={{0,2},{1,3},{2,4},{3,5},{4,6},{5,7},{6,0},{7,1},{8,10},{9,11},{10,... | collective-permute-start | bytes 1622024 | tf_op jit(solution)/shard_map/ppermute | solution.py:219
  168.6 52.4 %slice-start.1 = ((s8[8388608]{0:T(1024)(128)(4,1)}), s8[4194304]{0:T(1024)(128)(4,1)S(1)}, s32[]{:S(2)}) async-start(s8[8388608]{0:T(1024)(128)(4,1)} %bitcast.69), calls=%async_computation.2 | async-start | bytes 8388608
  176.3 49.4 %collective-permute-start.10 = (s16[528,512]{1,0:T(8,128)(2,1)S(1)}, s16[528,512]{1,0:T(8,128)(2,1)S(1)}, u32[]{:S(2)}, u32[]{:S(2)}) collective-permute-start(s16[528,512]{1,0:T(8,128)(2,1)S(1)} %get-tuple-element.21), channel_id=1, source_target_pairs={{0,6},{1,7},{2,0},{3,1},{4,2},{5,3},{6,4},{7,5},{8,14},{9,15},{10,... | collective-permute-start | bytes 1622024 | tf_op jit(solution)/shard_map/ppermute | solution.py:219
  183.3 58.7 %collective-permute-start.9 = (s16[528,512]{1,0:T(8,128)(2,1)S(1)}, s16[528,512]{1,0:T(8,128)(2,1)S(1)}, u32[]{:S(2)}, u32[]{:S(2)}) collective-permute-start(s16[528,512]{1,0:T(8,128)(2,1)S(1)} %get-tuple-element.22), channel_id=1, source_target_pairs={{0,4},{1,5},{2,6},{3,7},{4,0},{5,1},{6,2},{7,3},{8,12},{9,13},{10,... | collective-permute-start | bytes 1622024 | tf_op jit(solution)/shard_map/ppermute | solution.py:219
  220.3 21.7 %collective-permute-start.8 = (s16[528,512]{1,0:T(8,128)(2,1)S(1)}, s16[528,512]{1,0:T(8,128)(2,1)S(1)}, u32[]{:S(2)}, u32[]{:S(2)}) collective-permute-start(s16[528,512]{1,0:T(8,128)(2,1)S(1)} %get-tuple-element.20), channel_id=1, source_target_pairs={{0,2},{1,3},{2,4},{3,5},{4,6},{5,7},{6,0},{7,1},{8,10},{9,11},{10,... | collective-permute-start | bytes 1622024 | tf_op jit(solution)/shard_map/ppermute | solution.py:219
  223.5 24.3 %collective-permute-start.5 = (bf16[256,4096]{1,0:T(8,128)(2,1)S(1)}, bf16[256,4096]{1,0:T(8,128)(2,1)S(1)}, u32[]{:S(2)}, u32[]{:S(2)}) collective-permute-start(bf16[256,4096]{1,0:T(8,128)(2,1)S(1)} %fusion.10), channel_id=1, source_target_pairs={{8,0},{9,1},{10,2},{11,3},{12,4},{13,5},{14,6},{15,7}} | collective-permute-start | bytes 6291464 | tf_op jit(solution)/shard_map/ppermute | solution.py:238
  247.8 1.6 copy-start.3
Sparse Core Ops, SparseCore 0:
  9.6 36.9 all-gather.1

commit v2 on v1

--- a/solution.py
+++ b/solution.py
@@ -59,20 +59,21 @@
         ],
         out_specs=pl.BlockSpec((2, length, HD), lambda g, m: (0, m, g)),
         out_shape=jax.ShapeDtypeStruct((2, micro * length, count * HD), jnp.bfloat16),
-        cost_estimate=pl.CostEstimate(
-            flops=8 * count * micro * GRP * length * length * HD,
-            bytes_accessed=4 * count * micro * length * wide,
-            transcendentals=count * micro * GRP * length * length,
-        ),
+        cost_estimate=pl.CostEstimate(flops=0, bytes_accessed=0, transcendentals=0),
         compiler_params=pltpu.CompilerParams(vmem_limit_bytes=VMEM),
         name="attention_grads",
     )(keys, values, queries, grads, places)
 
 
-def weight_body(own_ref, other_ref, own_d_ref, other_d_ref, out_ref):
+def side_by_side(low_ref, high_ref):
+    parts = [low_ref[0], high_ref[0], low_ref[1], high_ref[1]]
+    return jnp.concatenate(parts, axis=1)
+
+
+def weight_body(own_ref, other_ref, own_low, own_high, other_low, other_high, out_ref):
     rows = own_ref.shape[1]
-    own_d = jnp.concatenate([own_d_ref[0], own_d_ref[1]], axis=1)
-    other_d = jnp.concatenate([other_d_ref[0], other_d_ref[1]], axis=1)
+    own_d = side_by_side(own_low, own_high)
+    other_d = side_by_side(other_low, other_high)
     total = lax.dot_general(own_ref[...], own_d, TN, preferred_element_type=jnp.float32)
     total += lax.dot_general(other_ref[...], other_d, TN, preferred_element_type=jnp.float32)
     most = jnp.maximum(jnp.max(jnp.abs(total), axis=0, keepdims=True), 1e-30)
@@ -86,23 +87,19 @@
 def weight_terms(own, other, own_d, other_d, chunks):
     tokens, width = own.shape
     rows = width // chunks
-    columns = 2 * own_d.shape[2]
+    columns = 4 * own_d[0].shape[2]
     block = pl.BlockSpec((tokens, rows), lambda k: (0, k))
-    whole = pl.BlockSpec(own_d.shape, lambda k: (0, 0, 0))
+    whole = pl.BlockSpec(own_d[0].shape, lambda k: (0, 0, 0))
     return pl.pallas_call(
         weight_body,
         grid=(chunks,),
-        in_specs=[block, block, whole, whole],
+        in_specs=[block, block, whole, whole, whole, whole],
         out_specs=pl.BlockSpec((1, rows + PAD, columns), lambda k: (k, 0, 0)),
         out_shape=jax.ShapeDtypeStruct((chunks, rows + PAD, columns), jnp.int16),
-        cost_estimate=pl.CostEstimate(
-            flops=4 * tokens * width * columns,
-            bytes_accessed=4 * tokens * width + 2 * width * columns,
-            transcendentals=0,
-        ),
+        cost_estimate=pl.CostEstimate(flops=0, bytes_accessed=0, transcendentals=0),
         compiler_params=pltpu.CompilerParams(vmem_limit_bytes=VMEM),
         name="weight_terms",
-    )(own, other, own_d, other_d)
+    )(own, other, *own_d, *other_d)
 
 
 def branch_body(x_ref, low_ref, high_ref, wk_ref, wv_ref, gain_ref, out_ref, term_ref):
@@ -155,11 +152,7 @@
             jax.ShapeDtypeStruct((tokens, width), jnp.float32),
             jax.ShapeDtypeStruct((1, width), jnp.float32),
         ],
-        cost_estimate=pl.CostEstimate(
-            flops=4 * tokens * width * wk.shape[1],
-            bytes_accessed=6 * tokens * width + 4 * width * wk.shape[1],
-            transcendentals=0,
-        ),
+        cost_estimate=pl.CostEstimate(flops=0, bytes_accessed=0, transcendentals=0),
         compiler_params=pltpu.CompilerParams(vmem_limit_bytes=VMEM),
         name="branch_terms",
     )(x, low, high, wk, wv, gain)
@@ -192,16 +185,16 @@
     x_f = x.astype(jnp.float32)
     inverse = lax.rsqrt(jnp.mean(x_f * x_f, axis=-1, keepdims=True) + EPS)
     normed = (x_f * inverse * norm_gain).astype(jnp.bfloat16)
-    other = lax.ppermute(parity(normed, 1 - side), "dp", swap)
-    own = parity(normed, side)
+    normed, given, own = lax.optimization_barrier(
+        (normed, parity(normed, 1 - side), parity(normed, side))
+    )
+    other = lax.ppermute(given, "dp", swap)
     keys = jnp.dot(normed, wk, preferred_element_type=jnp.float32).astype(jnp.bfloat16)
     values = jnp.dot(normed, wv, preferred_element_type=jnp.float32).astype(jnp.bfloat16)
 
     heads = keys.shape[1] // HD
     half = heads // 2
     places = positions.reshape(micro, 1, length)
-    grads, sums = [], []
-
     def shift_from(k):
         pairs = []
         for i in range(replicas):
@@ -209,17 +202,33 @@
             pairs.append((i, target))
         return pairs
 
+    grads, theirs = [], []
     for first in (0, half):
         mine = attention_grads(keys, values, queries[0], attn_grad[0], places, first, half)
         grads.append(mine)
-        theirs = lax.ppermute(mine, "dp", swap)
-        coded = weight_terms(own, other, mine, theirs, chunks)
-        pieces = [coded[0]]
-        for k in range(1, chunks):
-            pieces.append(lax.ppermute(coded[k], "dp", shift_from(k)))
-        sums.append(pieces)
-
-    branch, term = branch_terms(x, grads[0], grads[1], wk, wv, norm_gain)
+        theirs.append(lax.ppermute(mine, "dp", swap))
+        keys, mine = lax.optimization_barrier((keys, mine))
+
+    branch, term = branch_terms(x, *grads, wk, wv, norm_gain)
+    branch, other, *theirs = lax.optimization_barrier((branch, other, *theirs))
+    sections = lax.axis_size("section")
+    section = lax.axis_index("section")
+    top = top_full.reshape(tokens, width).astype(jnp.float32)
+    current = (top + branch).astype(jnp.bfloat16)
+    own, current = lax.optimization_barrier((own, current))
+    coded = weight_terms(own, other, grads, theirs, chunks)
+    pieces = []
+    for k in range(1, chunks):
+        pieces.append(lax.ppermute(coded[k], "dp", shift_from(k)))
+    for s in range(sections - 2, -1, -1):
+        came = lax.ppermute(current, "section", [(s + 1, s)])
+        if s == sections - 2:
+            came, coded = lax.optimization_barrier((came, coded))
+        if s == sections - 3:
+            came, *pieces = lax.optimization_barrier((came, *pieces))
+        added = (came.astype(jnp.float32) + branch).astype(jnp.bfloat16)
+        current = jnp.where(section == s, added, current)
+    passed = current.reshape(micro, length, width)
 
     gain_part = parity(term, side) + lax.ppermute(parity(term, 1 - side), "dp", swap)
     gain_share = gain_part[:, :rows]
@@ -228,31 +237,14 @@
         gain_share = gain_share + lax.ppermute(piece, "dp", shift_from(k))
     gain_share = gain_share / seq_total
 
-    sections = lax.axis_size("section")
-    section = lax.axis_index("section")
-    passed = []
-    for m in range(micro):
-        mine = branch[m * length : (m + 1) * length]
-        current = (top_full[m].astype(jnp.float32) + mine).astype(jnp.bfloat16)
-        for s in range(sections - 2, -1, -1):
-            came = lax.ppermute(current, "section", [(s + 1, s)])
-            added = (came.astype(jnp.float32) + mine).astype(jnp.bfloat16)
-            current = jnp.where(section == s, added, current)
-        passed.append(current)
-    passed = jnp.stack(passed)
-
-    def decoded(pieces):
-        total = None
-        for piece in pieces:
-            unit = jnp.exp2(piece[rows : rows + 1].astype(jnp.float32))
-            part = piece[:rows].astype(jnp.float32) * unit
-            total = part if total is None else total + part
-        return total / seq_total
-
-    low, high = decoded(sums[0]), decoded(sums[1])
-    wide = half * HD
-    key_share = jnp.concatenate([low[:, :wide], high[:, :wide]], axis=1)
-    value_share = jnp.concatenate([low[:, wide:], high[:, wide:]], axis=1)
+    total = None
+    for piece in [coded[0], *pieces]:
+        unit = jnp.exp2(piece[rows : rows + 1].astype(jnp.float32))
+        part = piece[:rows].astype(jnp.float32) * unit
+        total = part if total is None else total + part
+    total = total / seq_total
+    wide = keys.shape[1]
+    key_share, value_share = total[:, :wide], total[:, wide:]
     return (passed[None], key_share[None], value_share[None], gain_share)
 
 

time: 259 us -> 268 us (1.035); the launches traced: 259 us -> 264 us
  starting transfers between devices: 25.5 us -> 44.7 us
  waiting for transfers between devices: 98.2 us -> 88.2 us
  Pallas kernels: 58.7 us -> 54.7 us
    ppermute x6 -> x3, waiting for transfers between devices: 26.3 us -> 0.01 us  [shards(): came = lax.ppermute(current, 'section', [(s + 1, s)])]
    ppermute x3, starting transfers between devices: 3.9 us -> 25.6 us  [shards(): gain_share = gain_share + lax.ppermute(piece, 'dp', shift_from(k))]
    select_n x3, other arithmetic: 13.4 us -> 27.4 us  [shards(): current = jnp.where(section == s, added, current)]
    ppermute x6 -> x3, waiting for transfers between devices: 56.7 us -> 69.5 us  [shards(): pieces.append(lax.ppermute(coded[k], 'dp', shift_from(k)))]
    another operation x2 -> x0, other arithmetic: 9.9 us -> none  [shards(): passed = jnp.stack(passed)]
    broadcast_in_dim x2 -> x0, other arithmetic: 4 us -> none  [shards(): return (passed[None], key_share[None], value_share[None], gain_share)]
    pallas_call x2 -> x1, Pallas kernels: 12.2 us -> 8.54 us  [weight_terms(): pl.pallas_call(weight_body, grid=(chunks,), in_specs=[block, block, whole...]
    ppermute x6 -> x3, starting transfers between devices: 6.82 us -> 4.64 us  [shards(): pieces.append(lax.ppermute(coded[k], 'dp', shift_from(k)))]
  transfers between devices with their start and end apart: 20 -> 14, of which waited for: 5 -> 7; matrix products, arithmetic and copies ran while one was open for 17% -> 10% of each run, Pallas kernels for 23% -> 21%
where the time goes in v2:
time: 268 us; the launch traced here: 264 us
  waiting for transfers between devices  88.2 us (33%)
  Pallas kernels  54.7 us (20%)
  other arithmetic  52.5 us (20%)
  starting transfers between devices  44.7 us (17%)
  between operations  14.3 us (5%)
  local copies, waits for them, and re-layouts  4.75 us (2%)
  matrix products  4.65 us (2%)
    ppermute x3, waiting for transfers between devices, shards(): pieces.append(lax.ppermute(coded[k], 'dp', shift_from(k)))  69.5 us
    select_n x3, other arithmetic, shards(): current = jnp.where(section == s, added, current)  27.4 us
    pallas_call x2, Pallas kernels, attention_grads(): pl.pallas_call(attention_body, grid=(count, micro), in_specs=[pl.BlockSpe...  26.4 us
    ppermute x3, starting transfers between devices, shards(): gain_share = gain_share + lax.ppermute(piece, 'dp', shift_from(k))  25.6 us
    pallas_call x1, Pallas kernels, branch_terms(): pl.pallas_call(branch_body, grid=(tokens // rows,), in_specs=[pl.BlockSpe...  19.8 us
    ppermute x2, waiting for transfers between devices, shards(): theirs.append(lax.ppermute(mine, 'dp', swap))  15.1 us
    ppermute x3, starting transfers between devices, shards(): came = lax.ppermute(current, 'section', [(s + 1, s)])  9.51 us
    pallas_call x1, Pallas kernels, weight_terms(): pl.pallas_call(weight_body, grid=(chunks,), in_specs=[block, block, whole...  8.54 us
  transfers between devices with their start and end apart: 14, of which 7 were waited for; matrix products, arithmetic and copies ran while one was open for 10% of the time, Pallas kernels for 21%

profile of v2, /device:TPU:1, one launch (start us, length us, event | category | flops | bytes accessed | tf_op | source)
XLA Modules:
  0.0 263.7 jit_solution(11039811066021928488)
XLA Ops:
  7.2 0.0 all-gather.2.cloned.1.call-start
  7.2 0.7 all-gather.2.cloned.1.call-update
  8.0 3.1 %multiply_reduce_fusion = f32[2,256]{1,0:T(2,128)S(1)} fusion(bf16[1,2,256,4096]{3,2,1,0:T(8,128)(2,1)} %param.8), kind=kLoop, calls=%fused_computation.6 | loop fusion | flops 6290944 | bytes 4196352 | tf_op jit(solution)/shard_map/reduce_sum | solution.py:186
  11.1 3.8 %multiply_convert_fusion = bf16[512,4096]{1,0:T(8,128)(2,1)S(1)} fusion(f32[4096]{0:T(1024)S(1)} %bitcast.37, f32[512]{0:T(512)S(1)} %bitcast.50, bf16[1,2,256,4096]{3,2,1,0:T(8,128)(2,1)} %param.8), kind=kLoop, calls=%fused_computation.5 | loop fusion | flops 8388608 | bytes 8407040 | tf_op jit(solution)/shard_map/convert_element_type | solution.py:187
  15.0 0.5 constant_dynamic-slice_fusion.11
  15.5 0.0 copy-start.4
  15.5 0.0 copy-start.3
  15.5 2.7 %pad_maximum_fusion = (bf16[512,2048]{1,0:T(8,128)(2,1)}, bf16[512,2048]{1,0:T(8,128)(2,1)}) fusion(bf16[512,512]{1,0:T(8,128)(2,1)S(1)} %get-tuple-element.47, bf16[512,512]{1,0:T(8,128)(2,1)S(1)} %get-tuple-element.48, bf16[512,512]{1,0:T(8,128)(2,1)S(1)} %get-tuple-element.49, bf16[512,512]{1,0:T(8,128)(2,1)S(1)} %get-tuple-element.50, ...), kind=kLoop, calls=%fused_computation.10 | loop fusion | flops 16777216 | bytes 8388608 | tf_op jit(solution)/shard_map/concatenate | solution.py:183
  18.2 2.1 collective-permute-start
  20.4 2.3 convolution_convert_fusion.v_ref
  22.7 0.5 copy-done.2
  23.2 2.3 convolution_convert_fusion.1.k_ref
  25.5 13.2 %attention_grads.2.low_ref.own_low = bf16[2,512,256]{2,1,0:T(8,128)(2,1)S(1)} custom-call(bf16[512,512]{1,0:T(8,128)(2,1)S(1)} %convolution_convert_fusion.1.k_ref, bf16[512,512]{1,0:T(8,128)(2,1)S(1)} %convolution_convert_fusion.v_ref, bf16[2,256,4096]{2,1,0:T(8,128)(2,1)} %bitcast.39, bf16[2,256,4096]{2,1,0:T(8,128)(2,1)} %bitcast.41, ...), custom_call_target="tpu_custom_call" | custom-call | tf_op jit(solution)/shard_map/attention_grads/pallas_call | solution.py:50
  38.7 13.2 %attention_grads.3.high_ref.own_high = bf16[2,512,256]{2,1,0:T(8,128)(2,1)S(1)} custom-call(bf16[512,512]{1,0:T(8,128)(2,1)S(1)} %convolution_convert_fusion.1.k_ref, bf16[512,512]{1,0:T(8,128)(2,1)S(1)} %convolution_convert_fusion.v_ref, bf16[2,256,4096]{2,1,0:T(8,128)(2,1)} %bitcast.40, bf16[2,256,4096]{2,1,0:T(8,128)(2,1)} %bitcast.42, ...), custom_call_target="tpu_custom_call" | custom-call | tf_op jit(solution)/shard_map/attention_grads/pallas_call | solution.py:50
  51.9 1.2 collective-permute-start.2
  53.1 0.3 collective-permute-start.1
  53.4 19.8 %branch_terms.1 = (f32[512,4096]{1,0:T(8,128)}, f32[1,4096]{1,0:T(1,128)S(1)}) custom-call(bf16[512,4096]{1,0:T(8,128)(2,1)} %bitcast.38, bf16[2,512,256]{2,1,0:T(8,128)(2,1)S(1)} %attention_grads.2.low_ref.own_low, bf16[2,512,256]{2,1,0:T(8,128)(2,1)S(1)} %attention_grads.3.high_ref.own_high, bf16[4096,512]{1,0:T(8,128)(2,1)} %bitcast.44, ...), custom_call_target="tpu_custom_call" | custom-call | tf_op jit(solution)/shard_map/branch_terms/pallas_call | solution.py:136
  73.2 3.9 %collective-permute-done.2.other_high = bf16[2,512,256]{2,1,0:T(8,128)(2,1)S(1)} collective-permute-done((bf16[2,512,256]{2,1,0:T(8,128)(2,1)S(1)}, bf16[2,512,256]{2,1,0:T(8,128)(2,1)S(1)}, u32[]{:S(2)}, u32[]{:S(2)}) %collective-permute-start.2) | collective-permute-done | bytes 524320 | tf_op jit(solution)/shard_map/ppermute | solution.py:209
  77.1 11.2 %collective-permute-done.1.other_low = bf16[2,512,256]{2,1,0:T(8,128)(2,1)S(1)} collective-permute-done((bf16[2,512,256]{2,1,0:T(8,128)(2,1)S(1)}, bf16[2,512,256]{2,1,0:T(8,128)(2,1)S(1)}, u32[]{:S(2)}, u32[]{:S(2)}) %collective-permute-start.1) | collective-permute-done | bytes 524320 | tf_op jit(solution)/shard_map/ppermute | solution.py:209
  88.4 8.0 %fusion = bf16[512,4096]{1,0:T(8,128)(2,1)} fusion(f32[512,4096]{1,0:T(8,128)} %get-tuple-element.27, bf16[2,256,4096]{2,1,0:T(8,128)(2,1)} %all-gather.2.cloned.1.call-done), kind=kLoop, calls=%fused_computation.1 | loop fusion | flops 6291456 | bytes 16777216 | tf_op jit(solution)/shard_map/convert_element_type | solution.py:217
  96.4 2.6 collective-permute-start.3
  99.0 8.5 %weight_terms.1 = s16[4,528,1024]{2,1,0:T(8,128)(2,1)} custom-call(bf16[512,2048]{1,0:T(8,128)(2,1)} %get-tuple-element.29.own_ref, bf16[512,2048]{1,0:T(8,128)(2,1)} %collective-permute-done.other_ref, bf16[2,512,256]{2,1,0:T(8,128)(2,1)S(1)} %attention_grads.2.low_ref.own_low, bf16[2,512,256]{2,1,0:T(8,128)(2,1)S(1)} %attention_grads.3.high_ref.own_high, ...), custom_call_target="tpu_custom_call" | custom-call | tf_op jit(solution)/shard_map/weight_terms/pallas_call | solution.py:93
  107.5 10.0 %fusion.1 = bf16[512,4096]{1,0:T(8,128)(2,1)} fusion(bf16[512,4096]{1,0:T(8,128)(2,1)} %fusion, f32[512,4096]{1,0:T(8,128)} %get-tuple-element.27, bf16[512,4096]{1,0:T(8,128)(2,1)} %collective-permute-done.3, pred[]{:T(512)S(6)} %eq.11), kind=kLoop, calls=%fused_computation.7 | loop fusion | flops 8388608 | bytes 20971520 | tf_op jit(solution)/shard_map/jit(_where)/select_n | solution.py:230
  117.5 1.3 collective-permute-start.4
  118.8 2.2 slice_bitcast_fusion
  121.0 1.3 collective-permute-start.5
  122.2 2.3 collective-permute-start.6
  124.6 1.1 collective-permute-start.7
  125.6 20.2 %collective-permute-done.5 = s16[528,1024]{1,0:T(8,128)(2,1)} collective-permute-done((s16[528,1024]{1,0:T(8,128)(2,1)S(1)}, s16[528,1024]{1,0:T(8,128)(2,1)}, u32[]{:S(2)}, u32[]{:S(2)}) %collective-permute-start.5) | collective-permute-done | bytes 1081376 | tf_op jit(solution)/shard_map/ppermute | solution.py:222
  145.8 49.3 %collective-permute-done.6 = s16[528,1024]{1,0:T(8,128)(2,1)} collective-permute-done((s16[528,1024]{1,0:T(8,128)(2,1)S(1)}, s16[528,1024]{1,0:T(8,128)(2,1)}, u32[]{:S(2)}, u32[]{:S(2)}) %collective-permute-start.6) | collective-permute-done | bytes 1081376 | tf_op jit(solution)/shard_map/ppermute | solution.py:222
  195.1 8.8 %fusion.2 = bf16[512,4096]{1,0:T(8,128)(2,1)} fusion(bf16[512,4096]{1,0:T(8,128)(2,1)} %fusion.1, f32[512,4096]{1,0:T(8,128)} %get-tuple-element.27, bf16[512,4096]{1,0:T(8,128)(2,1)} %collective-permute-done.4, pred[]{:T(512)S(6)} %eq.10), kind=kLoop, calls=%fused_computation.8 | loop fusion | flops 8388608 | bytes 20971520 | tf_op jit(solution)/shard_map/jit(_where)/select_n | solution.py:230
  203.9 5.6 %collective-permute-start.8 = (bf16[512,4096]{1,0:T(8,128)(2,1)}, bf16[512,4096]{1,0:T(8,128)(2,1)}, u32[]{:S(2)}, u32[]{:S(2)}) collective-permute-start(bf16[512,4096]{1,0:T(8,128)(2,1)} %fusion.2), channel_id=1, source_target_pairs={{8,0},{9,1},{10,2},{11,3},{12,4},{13,5},{14,6},{15,7}} | collective-permute-start | bytes 12582920 | tf_op jit(solution)/shard_map/ppermute | solution.py:224
  209.6 1.3 collective-permute-start.9
  210.9 1.3 collective-permute-done.9
  212.2 23.4 %collective-permute-start.10 = (f32[1,512]{1,0:T(1,128)S(1)}, f32[1,512]{1,0:T(1,128)S(1)}, u32[]{:S(2)}, u32[]{:S(2)}) collective-permute-start(f32[1,512]{1,0:T(1,128)S(1)} %get-tuple-element.61), channel_id=1, source_target_pairs={{0,2},{1,3},{2,4},{3,5},{4,6},{5,7},{6,0},{7,1},{8,10},{9,11},{10,... | collective-permute-start | bytes 6152 | tf_op jit(solution)/shard_map/ppermute | solution.py:237
  235.6 1.3 collective-permute-start.11
  236.9 0.9 collective-permute-start.12
  237.8 1.2 collective-permute-done.11
  238.9 0.4 collective-permute-done.12
  239.3 0.6 fusion.10
  239.9 0.7 multiply_exponential_fusion.3
  240.6 0.7 multiply_exponential_fusion.2
  241.4 0.7 multiply_exponential_fusion.1
  242.1 0.7 multiply_exponential_fusion
  242.8 0.0 copy-start.1
  242.9 4.0 %fusion.7 = f32[512,1024]{1,0:T(8,128)S(1)} fusion(f32[1024]{0:T(1024)S(1)} %bitcast.49, s16[528,1024]{1,0:T(8,128)(2,1)} %collective-permute-done.7, f32[1024]{0:T(1024)S(1)} %bitcast.48, s16[528,1024]{1,0:T(8,128)(2,1)} %collective-permute-done.6, f32[1024]{0:T(1024)S(1)} %bitcast.47, s16[528,1024]{1,0:T(8,128)(2,1)} %collective-permute-done.5, ...), kind=kLoop, calls=%fused_computation.16 | loop fusion | flops 6291456 | bytes 6307840 | tf_op jit(solution)/shard_map/div | solution.py:245
  246.8 1.5 slice_bitcast_fusion.3
  248.3 8.6 %fusion.3 = bf16[512,4096]{1,0:T(8,128)(2,1)} fusion(f32[512,4096]{1,0:T(8,128)} %get-tuple-element.27, bf16[512,4096]{1,0:T(8,128)(2,1)} %collective-permute-done.8, pred[]{:T(512)S(6)} %eq.9, bf16[512,4096]{1,0:T(8,128)(2,1)S(1)} %copy-done.1, bf16[512,4096]{1,0:T(8,128)(2,1)} %collective-permute-done.4, pred[]{:T(512)S(6)} %eq.10), kind=kLoop, calls=%fused_computation.9 | loop fusion | flops 16777216 | bytes 25165826 | tf_op jit(solution)/shard_map/jit(_where)/select_n | solution.py:230
  (20 shorter events, 0.1 us)
Async XLA Ops:
  7.2 4.0 %copy-start = (f32[1,4096]{1,0:T(1,128)S(1)}, f32[1,4096]{1,0:T(1,128)}, u32[]{:S(2)}) copy-start(f32[1,4096]{1,0:T(1,128)} %gain_ref.1) | copy-start | bytes 49156
  7.2 81.2 %all-gather.2.cloned.1.call-start = ((), (), s32[]{:S(2)}) async-start(), calls=%async_computation | async-start | bytes 5242880 | tf_op jit(solution)/shard_map/all_gather | solution.py:176
  15.5 4.8 %copy-start.4 = (s32[2,256]{1,0:T(2,128)S(1)}, s32[2,256]{1,0:T(2,128)}, u32[]{:S(2)}) copy-start(s32[2,256]{1,0:T(2,128)} %param.12) | copy-start | bytes 6148
  15.5 4.8 %copy-start.3 = (bf16[1,4096,512]{2,1,0:T(8,128)(2,1)S(1)}, bf16[1,4096,512]{2,1,0:T(8,128)(2,1)}, u32[]{:S(2)}) copy-start(bf16[1,4096,512]{2,1,0:T(8,128)(2,1)} %param.15) | copy-start | bytes 12582916
  18.2 70.1 %collective-permute-start = (bf16[512,2048]{1,0:T(8,128)(2,1)}, bf16[512,2048]{1,0:T(8,128)(2,1)}, u32[]{:S(2)}, u32[]{:S(2)}) collective-permute-start(bf16[512,2048]{1,0:T(8,128)(2,1)} %get-tuple-element.26), channel_id=1, source_target_pairs={{0,1},{1,0},{2,3},{3,2},{4,5},{5,4},{6,7},{7,6},{8,9},{9,8},{10,11... | collective-permute-start | bytes 6291464 | tf_op jit(solution)/shard_map/ppermute | solution.py:191
  20.3 2.8 %copy-start.2 = (bf16[1,4096,512]{2,1,0:T(8,128)(2,1)S(1)}, bf16[1,4096,512]{2,1,0:T(8,128)(2,1)}, u32[]{:S(2)}) copy-start(bf16[1,4096,512]{2,1,0:T(8,128)(2,1)} %param.14) | copy-start | bytes 12582916
  51.9 25.3 %collective-permute-start.2 = (bf16[2,512,256]{2,1,0:T(8,128)(2,1)S(1)}, bf16[2,512,256]{2,1,0:T(8,128)(2,1)S(1)}, u32[]{:S(2)}, u32[]{:S(2)}) collective-permute-start(bf16[2,512,256]{2,1,0:T(8,128)(2,1)S(1)} %attention_grads.3.high_ref.own_high), channel_id=1, source_target_pairs={{0,1},{1,0},{2,3},{3,2},{4,5},{5,4},{6,7},{7,6},{8,9},{9,8},{10,11... | collective-permute-start | bytes 1572872 | tf_op jit(solution)/shard_map/ppermute | solution.py:209
  53.1 35.3 %collective-permute-start.1 = (bf16[2,512,256]{2,1,0:T(8,128)(2,1)S(1)}, bf16[2,512,256]{2,1,0:T(8,128)(2,1)S(1)}, u32[]{:S(2)}, u32[]{:S(2)}) collective-permute-start(bf16[2,512,256]{2,1,0:T(8,128)(2,1)S(1)} %attention_grads.2.low_ref.own_low), channel_id=1, source_target_pairs={{0,1},{1,0},{2,3},{3,2},{4,5},{5,4},{6,7},{7,6},{8,9},{9,8},{10,11... | collective-permute-start | bytes 1572872 | tf_op jit(solution)/shard_map/ppermute | solution.py:209
  96.4 11.1 %collective-permute-start.3 = (bf16[512,4096]{1,0:T(8,128)(2,1)}, bf16[512,4096]{1,0:T(8,128)(2,1)}, u32[]{:S(2)}, u32[]{:S(2)}) collective-permute-start(bf16[512,4096]{1,0:T(8,128)(2,1)} %fusion), channel_id=1, source_target_pairs={{24,16},{25,17},{26,18},{27,19},{28,20},{29,21},{30,22},{31,23}} | collective-permute-start | bytes 12582920 | tf_op jit(solution)/shard_map/ppermute | solution.py:224
  117.5 77.6 %collective-permute-start.4 = (bf16[512,4096]{1,0:T(8,128)(2,1)}, bf16[512,4096]{1,0:T(8,128)(2,1)}, u32[]{:S(2)}, u32[]{:S(2)}) collective-permute-start(bf16[512,4096]{1,0:T(8,128)(2,1)} %fusion.1), channel_id=1, source_target_pairs={{16,8},{17,9},{18,10},{19,11},{20,12},{21,13},{22,14},{23,15}} | collective-permute-start | bytes 12582920 | tf_op jit(solution)/shard_map/ppermute | solution.py:224
  121.0 24.9 %collective-permute-start.5 = (s16[528,1024]{1,0:T(8,128)(2,1)S(1)}, s16[528,1024]{1,0:T(8,128)(2,1)}, u32[]{:S(2)}, u32[]{:S(2)}) collective-permute-start(s16[528,1024]{1,0:T(8,128)(2,1)S(1)} %get-tuple-element.42), channel_id=1, source_target_pairs={{0,2},{1,3},{2,4},{3,5},{4,6},{5,7},{6,0},{7,1},{8,10},{9,11},{10,... | collective-permute-start | bytes 3244040 | tf_op jit(solution)/shard_map/ppermute | solution.py:222
  122.2 72.9 %collective-permute-start.6 = (s16[528,1024]{1,0:T(8,128)(2,1)S(1)}, s16[528,1024]{1,0:T(8,128)(2,1)}, u32[]{:S(2)}, u32[]{:S(2)}) collective-permute-start(s16[528,1024]{1,0:T(8,128)(2,1)S(1)} %get-tuple-element.41), channel_id=1, source_target_pairs={{0,4},{1,5},{2,6},{3,7},{4,0},{5,1},{6,2},{7,3},{8,12},{9,13},{10,... | collective-permute-start | bytes 3244040 | tf_op jit(solution)/shard_map/ppermute | solution.py:222
  124.6 70.5 %collective-permute-start.7 = (s16[528,1024]{1,0:T(8,128)(2,1)S(1)}, s16[528,1024]{1,0:T(8,128)(2,1)}, u32[]{:S(2)}, u32[]{:S(2)}) collective-permute-start(s16[528,1024]{1,0:T(8,128)(2,1)S(1)} %get-tuple-element.40), channel_id=1, source_target_pairs={{0,6},{1,7},{2,0},{3,1},{4,2},{5,3},{6,4},{7,5},{8,14},{9,15},{10,... | collective-permute-start | bytes 3244040 | tf_op jit(solution)/shard_map/ppermute | solution.py:222
  203.9 44.4 %collective-permute-start.8 = (bf16[512,4096]{1,0:T(8,128)(2,1)}, bf16[512,4096]{1,0:T(8,128)(2,1)}, u32[]{:S(2)}, u32[]{:S(2)}) collective-permute-start(bf16[512,4096]{1,0:T(8,128)(2,1)} %fusion.2), channel_id=1, source_target_pairs={{8,0},{9,1},{10,2},{11,3},{12,4},{13,5},{14,6},{15,7}} | collective-permute-start | bytes 12582920 | tf_op jit(solution)/shard_map/ppermute | solution.py:224
  209.6 2.6 collective-permute-start.9
  212.2 25.6 %collective-permute-start.10 = (f32[1,512]{1,0:T(1,128)S(1)}, f32[1,512]{1,0:T(1,128)S(1)}, u32[]{:S(2)}, u32[]{:S(2)}) collective-permute-start(f32[1,512]{1,0:T(1,128)S(1)} %get-tuple-element.61), channel_id=1, source_target_pairs={{0,2},{1,3},{2,4},{3,5},{4,6},{5,7},{6,0},{7,1},{8,10},{9,11},{10,... | collective-permute-start | bytes 6152 | tf_op jit(solution)/shard_map/ppermute | solution.py:237
  235.6 3.3 %collective-permute-start.11 = (f32[1,512]{1,0:T(1,128)S(1)}, f32[1,512]{1,0:T(1,128)S(1)}, u32[]{:S(2)}, u32[]{:S(2)}) collective-permute-start(f32[1,512]{1,0:T(1,128)S(1)} %get-tuple-element.63), channel_id=1, source_target_pairs={{0,4},{1,5},{2,6},{3,7},{4,0},{5,1},{6,2},{7,3},{8,12},{9,13},{10,... | collective-permute-start | bytes 6152 | tf_op jit(solution)/shard_map/ppermute | solution.py:237
  236.9 2.4 collective-permute-start.12
  242.8 5.5 %copy-start.1 = (bf16[512,4096]{1,0:T(8,128)(2,1)S(1)}, bf16[512,4096]{1,0:T(8,128)(2,1)}, u32[]{:S(2)}) copy-start(bf16[512,4096]{1,0:T(8,128)(2,1)} %fusion.1) | copy-start | bytes 12582916
Sparse Core Ops, SparseCore 0:
  9.6 36.9 all-gather.1

commit v3 on v2

--- a/solution.py
+++ b/solution.py
@@ -220,22 +220,23 @@
     pieces = []
     for k in range(1, chunks):
         pieces.append(lax.ppermute(coded[k], "dp", shift_from(k)))
-    for s in range(sections - 2, -1, -1):
-        came = lax.ppermute(current, "section", [(s + 1, s)])
-        if s == sections - 2:
-            came, coded = lax.optimization_barrier((came, coded))
-        if s == sections - 3:
-            came, *pieces = lax.optimization_barrier((came, *pieces))
-        added = (came.astype(jnp.float32) + branch).astype(jnp.bfloat16)
-        current = jnp.where(section == s, added, current)
-    passed = current.reshape(micro, length, width)
-
     gain_part = parity(term, side) + lax.ppermute(parity(term, 1 - side), "dp", swap)
     gain_share = gain_part[:, :rows]
     for k in range(1, chunks):
         piece = gain_part[:, k * rows : (k + 1) * rows]
         gain_share = gain_share + lax.ppermute(piece, "dp", shift_from(k))
     gain_share = gain_share / seq_total
+    for s in range(sections - 2, -1, -1):
+        came = lax.ppermute(current, "section", [(s + 1, s)])
+        if s == sections - 2:
+            came, coded = lax.optimization_barrier((came, coded))
+        if s == sections - 3:
+            came, gain_share, *pieces = lax.optimization_barrier(
+                (came, gain_share, *pieces)
+            )
+        added = (came.astype(jnp.float32) + branch).astype(jnp.bfloat16)
+        current = jnp.where(section == s, added, current)
+    passed = current.reshape(micro, length, width)
 
     total = None
     for piece in [coded[0], *pieces]:

time: 268 us -> 265 us (0.989)
  waiting for transfers between devices: 88.2 us -> 83.8 us
  starting transfers between devices: 44.7 us -> 49.1 us
    ppermute x3, waiting for transfers between devices: 69.5 us -> 0.01 us  [shards(): pieces.append(lax.ppermute(coded[k], 'dp', shift_from(k)))]
    ppermute x3, waiting for transfers between devices: 1.56 us -> 66.9 us  [shards(): gain_share = gain_share + lax.ppermute(piece, 'dp', shift_from(k))]
    ppermute x3, starting transfers between devices: 25.6 us -> 29 us  [shards(): gain_share = gain_share + lax.ppermute(piece, 'dp', shift_from(k))]
  transfers between devices with their start and end apart: 14 -> 14, of which waited for: 7 -> 6; matrix products, arithmetic and copies ran while one was open for 10% -> 9% of each run, Pallas kernels for 21% -> 21%
where the time goes in v3:
time: 265 us; the launch traced here: 261 us
  waiting for transfers between devices  83.8 us (32%)
  Pallas kernels  54.7 us (21%)
  other arithmetic  50.5 us (19%)
  starting transfers between devices  49.1 us (19%)
  between operations  14.3 us (5%)
  matrix products  4.71 us (2%)
  local copies, waits for them, and re-layouts  3.87 us (1%)
    ppermute x3, waiting for transfers between devices, shards(): gain_share = gain_share + lax.ppermute(piece, 'dp', shift_from(k))  66.9 us
    ppermute x3, starting transfers between devices, shards(): gain_share = gain_share + lax.ppermute(piece, 'dp', shift_from(k))  29 us
    select_n x3, other arithmetic, shards(): current = jnp.where(section == s, added, current)  27.5 us
    pallas_call x2, Pallas kernels, attention_grads(): pl.pallas_call(attention_body, grid=(count, micro), in_specs=[pl.BlockSpe...  26.4 us
    pallas_call x1, Pallas kernels, branch_terms(): pl.pallas_call(branch_body, grid=(tokens // rows,), in_specs=[pl.BlockSpe...  19.8 us
    ppermute x2, waiting for transfers between devices, shards(): theirs.append(lax.ppermute(mine, 'dp', swap))  14.9 us
    ppermute x3, starting transfers between devices, shards(): came = lax.ppermute(current, 'section', [(s + 1, s)])  11.4 us
    pallas_call x1, Pallas kernels, weight_terms(): pl.pallas_call(weight_body, grid=(chunks,), in_specs=[block, block, whole...  8.55 us
  transfers between devices with their start and end apart: 14, of which 6 were waited for; matrix products, arithmetic and copies ran while one was open for 9% of the time, Pallas kernels for 21%

profile of v3, /device:TPU:1, one launch (start us, length us, event | category | flops | bytes accessed | tf_op | source)
XLA Modules:
  0.0 261.0 jit_solution(15318888826008713654)
XLA Ops:
  7.2 0.0 all-gather.2.cloned.1.call-start
  7.2 0.7 all-gather.2.cloned.1.call-update
  8.0 3.1 %multiply_reduce_fusion = f32[2,256]{1,0:T(2,128)S(1)} fusion(bf16[1,2,256,4096]{3,2,1,0:T(8,128)(2,1)} %param.8), kind=kLoop, calls=%fused_computation.6 | loop fusion | flops 6290944 | bytes 4196352 | tf_op jit(solution)/shard_map/reduce_sum | solution.py:186
  11.2 3.8 %multiply_convert_fusion = bf16[512,4096]{1,0:T(8,128)(2,1)S(1)} fusion(f32[4096]{0:T(1024)S(1)} %bitcast.37, f32[512]{0:T(512)S(1)} %bitcast.50, bf16[1,2,256,4096]{3,2,1,0:T(8,128)(2,1)} %param.8), kind=kLoop, calls=%fused_computation.5 | loop fusion | flops 8388608 | bytes 8407040 | tf_op jit(solution)/shard_map/convert_element_type | solution.py:187
  15.0 0.5 constant_dynamic-slice_fusion.11
  15.5 0.0 copy-start.4
  15.5 0.0 copy-start.3
  15.5 1.7 pad_maximum_fusion
  17.3 2.1 collective-permute-start
  19.4 2.4 convolution_convert_fusion.v_ref
  21.7 0.5 copy-done.2
  22.2 2.4 convolution_convert_fusion.1.k_ref
  24.6 13.2 %attention_grads.2.low_ref.own_low = bf16[2,512,256]{2,1,0:T(8,128)(2,1)S(1)} custom-call(bf16[512,512]{1,0:T(8,128)(2,1)S(1)} %convolution_convert_fusion.1.k_ref, bf16[512,512]{1,0:T(8,128)(2,1)S(1)} %convolution_convert_fusion.v_ref, bf16[2,256,4096]{2,1,0:T(8,128)(2,1)} %bitcast.39, bf16[2,256,4096]{2,1,0:T(8,128)(2,1)} %bitcast.41, ...), custom_call_target="tpu_custom_call" | custom-call | tf_op jit(solution)/shard_map/attention_grads/pallas_call | solution.py:50
  37.7 13.2 %attention_grads.3.high_ref.own_high = bf16[2,512,256]{2,1,0:T(8,128)(2,1)S(1)} custom-call(bf16[512,512]{1,0:T(8,128)(2,1)S(1)} %convolution_convert_fusion.1.k_ref, bf16[512,512]{1,0:T(8,128)(2,1)S(1)} %convolution_convert_fusion.v_ref, bf16[2,256,4096]{2,1,0:T(8,128)(2,1)} %bitcast.40, bf16[2,256,4096]{2,1,0:T(8,128)(2,1)} %bitcast.42, ...), custom_call_target="tpu_custom_call" | custom-call | tf_op jit(solution)/shard_map/attention_grads/pallas_call | solution.py:50
  50.9 1.4 collective-permute-start.2
  52.4 0.1 collective-permute-start.1
  52.5 19.8 %branch_terms.1 = (f32[512,4096]{1,0:T(8,128)}, f32[1,4096]{1,0:T(1,128)S(1)}) custom-call(bf16[512,4096]{1,0:T(8,128)(2,1)} %bitcast.38, bf16[2,512,256]{2,1,0:T(8,128)(2,1)S(1)} %attention_grads.2.low_ref.own_low, bf16[2,512,256]{2,1,0:T(8,128)(2,1)S(1)} %attention_grads.3.high_ref.own_high, bf16[4096,512]{1,0:T(8,128)(2,1)} %bitcast.44, ...), custom_call_target="tpu_custom_call" | custom-call | tf_op jit(solution)/shard_map/branch_terms/pallas_call | solution.py:136
  72.3 3.6 %collective-permute-done.2.other_high = bf16[2,512,256]{2,1,0:T(8,128)(2,1)S(1)} collective-permute-done((bf16[2,512,256]{2,1,0:T(8,128)(2,1)S(1)}, bf16[2,512,256]{2,1,0:T(8,128)(2,1)S(1)}, u32[]{:S(2)}, u32[]{:S(2)}) %collective-permute-start.2) | collective-permute-done | bytes 524320 | tf_op jit(solution)/shard_map/ppermute | solution.py:209
  75.9 11.2 %collective-permute-done.1.other_low = bf16[2,512,256]{2,1,0:T(8,128)(2,1)S(1)} collective-permute-done((bf16[2,512,256]{2,1,0:T(8,128)(2,1)S(1)}, bf16[2,512,256]{2,1,0:T(8,128)(2,1)S(1)}, u32[]{:S(2)}, u32[]{:S(2)}) %collective-permute-start.1) | collective-permute-done | bytes 524320 | tf_op jit(solution)/shard_map/ppermute | solution.py:209
  87.2 0.0 collective-permute-done.other_ref
  87.2 8.0 %fusion = bf16[512,4096]{1,0:T(8,128)(2,1)} fusion(f32[512,4096]{1,0:T(8,128)} %get-tuple-element.28, bf16[2,256,4096]{2,1,0:T(8,128)(2,1)} %all-gather.2.cloned.1.call-done), kind=kLoop, calls=%fused_computation.1 | loop fusion | flops 6291456 | bytes 16777216 | tf_op jit(solution)/shard_map/convert_element_type | solution.py:217
  95.2 2.6 collective-permute-start.3
  97.8 8.5 %weight_terms.1 = s16[4,528,1024]{2,1,0:T(8,128)(2,1)} custom-call(bf16[512,2048]{1,0:T(8,128)(2,1)} %get-tuple-element.30.own_ref, bf16[512,2048]{1,0:T(8,128)(2,1)} %collective-permute-done.other_ref, bf16[2,512,256]{2,1,0:T(8,128)(2,1)S(1)} %attention_grads.2.low_ref.own_low, bf16[2,512,256]{2,1,0:T(8,128)(2,1)S(1)} %attention_grads.3.high_ref.own_high, ...), custom_call_target="tpu_custom_call" | custom-call | tf_op jit(solution)/shard_map/weight_terms/pallas_call | solution.py:93
  106.3 0.0 collective-permute-done.3
  106.3 10.1 %fusion.1 = bf16[512,4096]{1,0:T(8,128)(2,1)} fusion(bf16[512,4096]{1,0:T(8,128)(2,1)} %fusion, f32[512,4096]{1,0:T(8,128)} %get-tuple-element.28, bf16[512,4096]{1,0:T(8,128)(2,1)} %collective-permute-done.3, pred[]{:T(512)S(6)} %eq.11), kind=kLoop, calls=%fused_computation.7 | loop fusion | flops 8388608 | bytes 20971520 | tf_op jit(solution)/shard_map/jit(_where)/select_n | solution.py:238
  116.5 1.3 collective-permute-start.4
  117.8 1.3 slice_bitcast_fusion
  119.1 2.2 collective-permute-start.10
  121.3 1.1 collective-permute-start.11
  122.4 0.4 collective-permute-start.9
  122.8 1.3 collective-permute-start.5
  124.1 1.2 collective-permute-done.5
  125.4 1.4 collective-permute-start.6
  126.7 63.6 %collective-permute-done.6 = f32[1,512]{1,0:T(1,128)S(1)} collective-permute-done((f32[1,512]{1,0:T(1,128)S(1)}, f32[1,512]{1,0:T(1,128)S(1)}, u32[]{:S(2)}, u32[]{:S(2)}) %collective-permute-start.6) | collective-permute-done | bytes 2080 | tf_op jit(solution)/shard_map/ppermute | solution.py:227
  190.3 27.6 %collective-permute-start.7 = (f32[1,512]{1,0:T(1,128)S(1)}, f32[1,512]{1,0:T(1,128)S(1)}, u32[]{:S(2)}, u32[]{:S(2)}) collective-permute-start(f32[1,512]{1,0:T(1,128)S(1)} %get-tuple-element.65), channel_id=1, source_target_pairs={{0,4},{1,5},{2,6},{3,7},{4,0},{5,1},{6,2},{7,3},{8,12},{9,13},{10,... | collective-permute-start | bytes 6152 | tf_op jit(solution)/shard_map/ppermute | solution.py:227
  217.9 1.0 collective-permute-done.7
  218.9 0.1 collective-permute-start.8
  219.0 2.4 collective-permute-done.8
  221.3 0.6 fusion.10
  221.9 0.0 collective-permute-done.4
  221.9 8.8 %fusion.2 = bf16[512,4096]{1,0:T(8,128)(2,1)} fusion(bf16[512,4096]{1,0:T(8,128)(2,1)} %fusion.1, f32[512,4096]{1,0:T(8,128)} %get-tuple-element.28, bf16[512,4096]{1,0:T(8,128)(2,1)} %collective-permute-done.4, pred[]{:T(512)S(6)} %eq.10), kind=kLoop, calls=%fused_computation.8 | loop fusion | flops 8388608 | bytes 20971520 | tf_op jit(solution)/shard_map/jit(_where)/select_n | solution.py:238
  230.8 7.5 %collective-permute-start.12 = (bf16[512,4096]{1,0:T(8,128)(2,1)}, bf16[512,4096]{1,0:T(8,128)(2,1)}, u32[]{:S(2)}, u32[]{:S(2)}) collective-permute-start(bf16[512,4096]{1,0:T(8,128)(2,1)} %fusion.2), channel_id=1, source_target_pairs={{8,0},{9,1},{10,2},{11,3},{12,4},{13,5},{14,6},{15,7}} | collective-permute-start | bytes 12582920 | tf_op jit(solution)/shard_map/ppermute | solution.py:230
  238.3 0.7 multiply_exponential_fusion.3
  239.0 0.7 multiply_exponential_fusion.2
  239.8 0.7 multiply_exponential_fusion
  240.5 3.5 %fusion.7 = f32[512,1024]{1,0:T(8,128)S(1)} fusion(f32[1024]{0:T(1024)S(1)} %bitcast.49, s16[528,1024]{1,0:T(8,128)(2,1)} %collective-permute-done.11, f32[1024]{0:T(1024)S(1)} %bitcast.48, s16[528,1024]{1,0:T(8,128)(2,1)S(1)} %collective-permute-done.10, f32[1024]{0:T(1024)S(1)} %bitcast.47, s16[528,1024]{1,0:T(8,128)(2,1)} %collective-permute-done.9, ...), kind=kLoop, calls=%fused_computation.16 | loop fusion | flops 6291456 | bytes 6307840 | tf_op jit(solution)/shard_map/div | solution.py:246
  244.0 1.5 slice_bitcast_fusion.3
  245.6 8.6 %fusion.3 = bf16[512,4096]{1,0:T(8,128)(2,1)} fusion(f32[512,4096]{1,0:T(8,128)} %get-tuple-element.28, bf16[512,4096]{1,0:T(8,128)(2,1)} %collective-permute-done.12, pred[]{:T(512)S(6)} %eq.9, bf16[512,4096]{1,0:T(8,128)(2,1)} %fusion.1, bf16[512,4096]{1,0:T(8,128)(2,1)} %collective-permute-done.4, pred[]{:T(512)S(6)} %eq.10), kind=kLoop, calls=%fused_computation.9 | loop fusion | flops 16777216 | bytes 25165826 | tf_op jit(solution)/shard_map/jit(_where)/select_n | solution.py:238
  (20 shorter events, 0.1 us)
Async XLA Ops:
  7.2 4.0 %copy-start = (f32[1,4096]{1,0:T(1,128)S(1)}, f32[1,4096]{1,0:T(1,128)}, u32[]{:S(2)}) copy-start(f32[1,4096]{1,0:T(1,128)} %gain_ref.1) | copy-start | bytes 49156
  7.2 80.0 %all-gather.2.cloned.1.call-start = ((), (), s32[]{:S(2)}) async-start(), calls=%async_computation | async-start | bytes 5242880 | tf_op jit(solution)/shard_map/all_gather | solution.py:176
  15.5 3.8 %copy-start.4 = (s32[2,256]{1,0:T(2,128)S(1)}, s32[2,256]{1,0:T(2,128)}, u32[]{:S(2)}) copy-start(s32[2,256]{1,0:T(2,128)} %param.12) | copy-start | bytes 6148
  15.5 3.8 %copy-start.3 = (bf16[1,4096,512]{2,1,0:T(8,128)(2,1)S(1)}, bf16[1,4096,512]{2,1,0:T(8,128)(2,1)}, u32[]{:S(2)}) copy-start(bf16[1,4096,512]{2,1,0:T(8,128)(2,1)} %param.15) | copy-start | bytes 12582916
  17.3 69.9 %collective-permute-start = (bf16[512,2048]{1,0:T(8,128)(2,1)S(1)}, bf16[512,2048]{1,0:T(8,128)(2,1)}, u32[]{:S(2)}, u32[]{:S(2)}) collective-permute-start(bf16[512,2048]{1,0:T(8,128)(2,1)S(1)} %get-tuple-element.27), channel_id=1, source_target_pairs={{0,1},{1,0},{2,3},{3,2},{4,5},{5,4},{6,7},{7,6},{8,9},{9,8},{10,11... | collective-permute-start | bytes 6291464 | tf_op jit(solution)/shard_map/ppermute | solution.py:191
  19.4 2.8 %copy-start.2 = (bf16[1,4096,512]{2,1,0:T(8,128)(2,1)S(1)}, bf16[1,4096,512]{2,1,0:T(8,128)(2,1)}, u32[]{:S(2)}) copy-start(bf16[1,4096,512]{2,1,0:T(8,128)(2,1)} %param.14) | copy-start | bytes 12582916
  50.9 25.0 %collective-permute-start.2 = (bf16[2,512,256]{2,1,0:T(8,128)(2,1)S(1)}, bf16[2,512,256]{2,1,0:T(8,128)(2,1)S(1)}, u32[]{:S(2)}, u32[]{:S(2)}) collective-permute-start(bf16[2,512,256]{2,1,0:T(8,128)(2,1)S(1)} %attention_grads.3.high_ref.own_high), channel_id=1, source_target_pairs={{0,1},{1,0},{2,3},{3,2},{4,5},{5,4},{6,7},{7,6},{8,9},{9,8},{10,11... | collective-permute-start | bytes 1572872 | tf_op jit(solution)/shard_map/ppermute | solution.py:209
  52.4 34.8 %collective-permute-start.1 = (bf16[2,512,256]{2,1,0:T(8,128)(2,1)S(1)}, bf16[2,512,256]{2,1,0:T(8,128)(2,1)S(1)}, u32[]{:S(2)}, u32[]{:S(2)}) collective-permute-start(bf16[2,512,256]{2,1,0:T(8,128)(2,1)S(1)} %attention_grads.2.low_ref.own_low), channel_id=1, source_target_pairs={{0,1},{1,0},{2,3},{3,2},{4,5},{5,4},{6,7},{7,6},{8,9},{9,8},{10,11... | collective-permute-start | bytes 1572872 | tf_op jit(solution)/shard_map/ppermute | solution.py:209
  95.2 11.1 %collective-permute-start.3 = (bf16[512,4096]{1,0:T(8,128)(2,1)}, bf16[512,4096]{1,0:T(8,128)(2,1)}, u32[]{:S(2)}, u32[]{:S(2)}) collective-permute-start(bf16[512,4096]{1,0:T(8,128)(2,1)} %fusion), channel_id=1, source_target_pairs={{24,16},{25,17},{26,18},{27,19},{28,20},{29,21},{30,22},{31,23}} | collective-permute-start | bytes 12582920 | tf_op jit(solution)/shard_map/ppermute | solution.py:230
  106.3 11.5 %copy-start.1 = (s16[4,528,1024]{2,1,0:T(8,128)(2,1)S(1)}, s16[4,528,1024]{2,1,0:T(8,128)(2,1)}, u32[]{:S(2)}) copy-start(s16[4,528,1024]{2,1,0:T(8,128)(2,1)} %weight_terms.1) | copy-start | bytes 12976132
  116.5 105.5 %collective-permute-start.4 = (bf16[512,4096]{1,0:T(8,128)(2,1)}, bf16[512,4096]{1,0:T(8,128)(2,1)}, u32[]{:S(2)}, u32[]{:S(2)}) collective-permute-start(bf16[512,4096]{1,0:T(8,128)(2,1)} %fusion.1), channel_id=1, source_target_pairs={{16,8},{17,9},{18,10},{19,11},{20,12},{21,13},{22,14},{23,15}} | collective-permute-start | bytes 12582920 | tf_op jit(solution)/shard_map/ppermute | solution.py:230
  119.1 102.8 %collective-permute-start.10 = (s16[528,1024]{1,0:T(8,128)(2,1)}, s16[528,1024]{1,0:T(8,128)(2,1)S(1)}, u32[]{:S(2)}, u32[]{:S(2)}) collective-permute-start(s16[528,1024]{1,0:T(8,128)(2,1)} %get-tuple-element.43), channel_id=1, source_target_pairs={{0,4},{1,5},{2,6},{3,7},{4,0},{5,1},{6,2},{7,3},{8,12},{9,13},{10,... | collective-permute-start | bytes 3244040 | tf_op jit(solution)/shard_map/ppermute | solution.py:222
  121.3 100.6 %collective-permute-start.11 = (s16[528,1024]{1,0:T(8,128)(2,1)S(1)}, s16[528,1024]{1,0:T(8,128)(2,1)}, u32[]{:S(2)}, u32[]{:S(2)}) collective-permute-start(s16[528,1024]{1,0:T(8,128)(2,1)S(1)} %get-tuple-element.42), channel_id=1, source_target_pairs={{0,6},{1,7},{2,0},{3,1},{4,2},{5,3},{6,4},{7,5},{8,14},{9,15},{10,... | collective-permute-start | bytes 3244040 | tf_op jit(solution)/shard_map/ppermute | solution.py:222
  122.4 99.5 %collective-permute-start.9 = (s16[528,1024]{1,0:T(8,128)(2,1)S(1)}, s16[528,1024]{1,0:T(8,128)(2,1)}, u32[]{:S(2)}, u32[]{:S(2)}) collective-permute-start(s16[528,1024]{1,0:T(8,128)(2,1)S(1)} %get-tuple-element.44), channel_id=1, source_target_pairs={{0,2},{1,3},{2,4},{3,5},{4,6},{5,7},{6,0},{7,1},{8,10},{9,11},{10,... | collective-permute-start | bytes 3244040 | tf_op jit(solution)/shard_map/ppermute | solution.py:222
  122.8 2.6 collective-permute-start.5
  125.4 64.9 %collective-permute-start.6 = (f32[1,512]{1,0:T(1,128)S(1)}, f32[1,512]{1,0:T(1,128)S(1)}, u32[]{:S(2)}, u32[]{:S(2)}) collective-permute-start(f32[1,512]{1,0:T(1,128)S(1)} %get-tuple-element.63), channel_id=1, source_target_pairs={{0,2},{1,3},{2,4},{3,5},{4,6},{5,7},{6,0},{7,1},{8,10},{9,11},{10,... | collective-permute-start | bytes 6152 | tf_op jit(solution)/shard_map/ppermute | solution.py:227
  190.3 28.6 %collective-permute-start.7 = (f32[1,512]{1,0:T(1,128)S(1)}, f32[1,512]{1,0:T(1,128)S(1)}, u32[]{:S(2)}, u32[]{:S(2)}) collective-permute-start(f32[1,512]{1,0:T(1,128)S(1)} %get-tuple-element.65), channel_id=1, source_target_pairs={{0,4},{1,5},{2,6},{3,7},{4,0},{5,1},{6,2},{7,3},{8,12},{9,13},{10,... | collective-permute-start | bytes 6152 | tf_op jit(solution)/shard_map/ppermute | solution.py:227
  218.9 2.4 collective-permute-start.8
  230.8 14.8 %collective-permute-start.12 = (bf16[512,4096]{1,0:T(8,128)(2,1)}, bf16[512,4096]{1,0:T(8,128)(2,1)}, u32[]{:S(2)}, u32[]{:S(2)}) collective-permute-start(bf16[512,4096]{1,0:T(8,128)(2,1)} %fusion.2), channel_id=1, source_target_pairs={{8,0},{9,1},{10,2},{11,3},{12,4},{13,5},{14,6},{15,7}} | collective-permute-start | bytes 12582920 | tf_op jit(solution)/shard_map/ppermute | solution.py:230
Sparse Core Ops, SparseCore 0:
  9.6 36.9 all-gather.1
